TPU v7x, 32 devices: a whole 2x2x4 slice. The times are simulated.
32 devices in a mesh: dp: 4 (over y, core), ty: 4 (over z), tx: 2 (over x).
Axes of the slice: x: 2, y: 2, z: 4, core: 2. Of those that a mesh axis runs over, the one named last changes fastest.
Arguments:
- features: bfloat16 [4, 256, 128, 128], P('dp', 'ty', 'tx'), may hold values from -6 to 6
- filter_one: bfloat16 [3, 3, 128, 128], P(None, None, None, 'dp'), may hold values from -0.1875 to 0.1875
- filter_two: bfloat16 [3, 3, 128, 128], P(None, None, None, 'dp'), may hold values from -0.1875 to 0.1875
- speedup: float32 [4, 256, 128], P('dp', 'ty', 'tx'), may hold values from 0.5 to 2
- land_mask: int32 [4, 256, 128], P('dp', 'ty', 'tx'), may hold values 0 or 1
- offsets: int32 [4, 2], P('dp'), may hold values from 0 to 1023
- upstream: bfloat16 [4, 256, 128, 128], P('dp', 'ty', 'tx'), may hold values from -6 to 6
Outputs:
- output: bfloat16 [4, 256, 128, 128], P('dp', 'ty', 'tx')
- grad_input: bfloat16 [4, 256, 128, 128], P('dp', 'ty', 'tx')
- grad_one: float32 [3, 3, 128, 128], P(None, None, None, 'dp')
- grad_two: float32 [3, 3, 128, 128], P(None, None, None, 'dp')
All inputs are finite; a program needn't handle non-finite values. No bound on the sum of `land_mask` on one device may be relied on, other than what follows from the above.
Results may differ from a plain program's by a relative error of at most 0.014.
Values may be sent and summed in bfloat16 or wider, within the bound.
No kernel may reach another device: no remote copies, remote signals or barrier semaphores. Data moves between devices by JAX's collectives and lax.ppermute only.
A program may use at most 64 MiB of HBM per device.

v0:
```python
import functools
import math

import jax
import jax.numpy as jnp
from jax import lax
from jax.experimental import pallas as pl
from jax.experimental.pallas import tpu as pltpu
from jax.sharding import PartitionSpec as P

F32 = jnp.float32
BF16 = jnp.bfloat16
RIM = 16
PAST = 8
CHUNK = 16
PLANES = 5
VMEM = pl.BlockSpec(memory_space=pltpu.VMEM)
HBM = pl.BlockSpec(memory_space=pltpu.HBM)
MIB = 1024 * 1024
SMALL = pltpu.CompilerParams(vmem_limit_bytes=8 * MIB)
MEDIUM = pltpu.CompilerParams(vmem_limit_bytes=16 * MIB)


def in_hbm(*arrays):
    return [pltpu.with_memory_space_constraint(array, pltpu.HBM) for array in arrays]


def is_odd(axis):
    return lax.rem(lax.axis_index(axis), 2) == 1


def kind_pairs(count, kind):
    return [(i, i + 1) for i in range(kind, count - 1, 2)]


def swaps(axis, sent):
    got = []
    for kind in reversed(range(len(sent))):
        pairs = [p for i, j in kind_pairs(lax.axis_size(axis), kind) for p in ((i, j), (j, i))]
        got.append(lax.ppermute(sent[kind], axis, pairs))
    return got[::-1]


def sides(axis, got):
    odd = is_odd(axis)
    first = got[0]
    second = got[1] if len(got) > 1 else jnp.zeros_like(first)
    return jnp.where(odd, first, second), jnp.where(odd, second, first)


def rim_of(before, after):
    channels = after[0].shape[1]
    at = lax.broadcasted_iota(jnp.int32, (RIM, channels), 0)
    rim = jnp.where(at == 0, after[0], 0.0)
    if after[1] is not None:
        rim = jnp.where(at == 1, after[1], rim)
    if before[0] is not None:
        rim = jnp.where(at == RIM - 2, before[0], rim)
    return jnp.where(at == RIM - 1, before[1], rim)


def factor_tile(line, channels):
    high = line.astype(BF16).astype(F32)
    low = (line - high).astype(BF16).astype(F32)
    line = jnp.concatenate([high, low, jnp.zeros((RIM - 2, line.shape[1]), F32)])
    past = channels - line.shape[1]
    return line if past == 0 else jnp.concatenate([line, jnp.zeros((RIM, past), F32)], axis=1)


def tx_sides(got, height):
    result = []
    for rows in sides("tx", [ref[...].astype(F32) for ref in got]):
        lines = [rows[n * height : (n + 1) * height] for n in range(4)]
        parts = jnp.transpose(rows[4 * height :])
        result.append((lines, parts[:height, 0:1] + parts[:height, 1:2]))
    return result


def two_parts(column, channels):
    high = column.astype(BF16).astype(F32)
    low = (column - high).astype(BF16).astype(F32)
    lane = lax.broadcasted_iota(jnp.int32, (column.shape[0], channels), 1)
    return jnp.where(lane == 0, high, jnp.where(lane == 1, low, 0.0))


def columns_kernel(kinds_tx, offsets, features, upstream, speedup, land, one, two, *rest):
    sent, rest = rest[:kinds_tx], rest[kinds_tx:]
    factor_ref, filters_ref, own_columns, spread, blocks, speed, mask, place, sems = rest
    _, height, breadth = speedup.shape
    channels = features.shape[3]
    taps = one.shape[0]
    ends = (pl.ds(0, RIM), pl.ds(breadth - RIM, RIM))
    moves = [(speedup, speed), (land, mask), (offsets, place)]
    moves += [
        (ref.at[0, :, ends[side], :], blocks.at[2 * array + side])
        for array, ref in enumerate((features, upstream))
        for side in range(2)
    ]
    moves += [(one, filters_ref.at[pl.ds(0, taps)]), (two, filters_ref.at[pl.ds(taps, taps)])]
    copies = [pltpu.make_async_copy(*move, sems.at[n]) for n, move in enumerate(moves)]
    for copy in copies:
        copy.start()
    for copy in copies[:3]:
        copy.wait()
    shape = (height, breadth)
    row = place[0, 0] + lax.axis_index("ty") * height + lax.broadcasted_iota(jnp.int32, shape, 0)
    col = place[0, 1] + lax.axis_index("tx") * breadth + lax.broadcasted_iota(jnp.int32, shape, 1)
    factor = jnp.where(mask[0] == 1, speed[0], jnp.float32(1.0))
    factor = factor / (1.0 + row.astype(F32) / 512.0) / (1.0 + col.astype(F32) / 1024.0)
    factor_ref[...] = factor
    odd = is_odd("tx")

    def column(at):
        return spread[pl.ds(at, height, stride=RIM), :]

    heads, tails = [], []
    for array in range(2):
        copies[3 + 2 * array].wait()
        spread[...] = blocks[2 * array].astype(F32).reshape(height * RIM, channels)
        heads += [column(0), column(1)]
        copies[4 + 2 * array].wait()
        spread[...] = blocks[2 * array + 1].astype(F32).reshape(height * RIM, channels)
        tails += [column(RIM - 2), column(RIM - 1)]
    across = jnp.transpose(factor)
    heads.append(factor_tile(across[:1], channels))
    tails.append(factor_tile(across[breadth - 1 :], channels))
    for plane in range(PLANES):
        rows = slice(plane * height, min((plane + 1) * height, sent[0].shape[0]))
        sent[0][rows] = jnp.where(odd, heads[plane], tails[plane]).astype(BF16)
        if kinds_tx == 2:
            sent[1][rows] = jnp.where(odd, tails[plane], heads[plane]).astype(BF16)
    for array in range(2):
        own_columns[2 * array] = heads[2 * array].astype(BF16)
        own_columns[2 * array + 1] = tails[2 * array + 1].astype(BF16)
    for copy in copies[7:]:
        copy.wait()


def rows_kernel(kinds_tx, edges, factor_ref, *rest):
    got, sent = rest[:kinds_tx], rest[kinds_tx:]
    height, breadth = factor_ref.shape
    channels = edges.shape[3]
    across = jnp.transpose(factor_ref[...])
    (before, factor_before), (after, factor_after) = tx_sides(got, height)

    def message(side, lines, edge):
        planes = []
        for array in range(2):
            for n, line in enumerate(lines):
                rim = rim_of(
                    [before[2 * array + i][line : line + 1] for i in range(2)],
                    [after[2 * array + i][line : line + 1] for i in range(2)],
                )
                planes.append(jnp.concatenate([edges[2 * array + side, n].astype(F32), rim]))
        own = two_parts(across[:, edge : edge + 1], channels)
        rim = rim_of(
            (None, two_parts(factor_before[edge : edge + 1], channels)),
            (two_parts(factor_after[edge : edge + 1], channels), None),
        )
        planes.append(jnp.concatenate([own, rim]))
        return planes

    heads = message(0, (0, 1), 0)
    tails = message(1, (height - 2, height - 1), height - 1)
    odd = is_odd("ty")
    for plane in range(PLANES):
        sent[0][plane] = jnp.where(odd, heads[plane], tails[plane]).astype(BF16)
        if len(sent) == 2:
            sent[1][plane] = jnp.where(odd, tails[plane], heads[plane]).astype(BF16)


def pair_weights(target, block_of):
    channels = target.shape[2] // 2
    for half in range(2):
        for s in range(2):
            for t in range(2):
                a = 2 * half + s - t
                for e in range(3):
                    block = block_of(a, e) if 0 <= a <= 2 else jnp.zeros((channels, channels), BF16)
                    at = (3 * s + e) * channels
                    target[half, at : at + channels, t * channels : (t + 1) * channels] = block


def store_taps(target, where, s, wide, width):
    channels = wide.shape[-1]
    axis = wide.ndim - 2
    for e in range(3):
        if e == 1:
            moved = wide
        else:
            moved = pltpu.roll(wide, 1 if e == 0 else wide.shape[axis] - 1, axis)
        moved = moved[..., :width, :].astype(BF16)
        target[where, :, (3 * s + e) * channels : (3 * s + e + 1) * channels] = moved


def pair_conv(source, weights, at, pairs):
    _, width, depth = source.shape
    upper = source[at : at + pairs].reshape(pairs * width, depth)
    lower = source[at + 1 : at + 1 + pairs].reshape(pairs * width, depth)
    return deep_product(upper, lower, weights)


def deep_product(upper, lower, weights):
    _, depth, lanes = weights.shape
    return jnp.dot(
        jnp.concatenate([upper, lower], axis=1),
        weights[...].reshape(2 * depth, lanes),
        preferred_element_type=F32,
    )


def outer(grads, source):
    return lax.dot_general(grads, source, (((0,), (0,)), ((), ())), preferred_element_type=F32)


def own_kernel(
    features, upstream, factor_ref, x6, u6, up2, factors, edge_factors, edges, cells, sems
):
    _, height, breadth, channels = features.shape
    arrays = (features, upstream)
    parts = sems.shape[1]
    rows = height // parts
    copies = [
        [
            pltpu.make_async_copy(
                ref.at[0, pl.ds(n * rows, rows)],
                cells.at[array, pl.ds(n * rows, rows)],
                sems.at[array, n],
            )
            for array, ref in enumerate(arrays)
        ]
        for n in range(parts)
    ]
    for pair in copies:
        for copy in pair:
            copy.start()
    across = jnp.transpose(factor_ref[...])
    for i in range(height):
        line = jnp.broadcast_to(across[:, i : i + 1], (breadth, channels))
        if i in (0, height - 1):
            edge_factors[min(i, 1)] = line
        else:
            factors[(i - 1) // 2, (i - 1) % 2] = line

    def spread(q, carry):
        for s in range(2):
            for array, target in enumerate((x6, u6)):
                line = cells[array, 2 * q + s]
                store_taps(target, q, s, line.astype(F32), breadth)
            up2[q, :, s * channels : (s + 1) * channels] = line
        return carry

    for n, pair in enumerate(copies):
        for copy in pair:
            copy.wait()
        lax.fori_loop(n * rows // 2, (n + 1) * rows // 2, spread, 0)
    for array in range(2):
        edges[2 * array] = cells[array, :2]
        edges[2 * array + 1] = cells[array, height - 2 :]


def activations(pre, grad, factor):
    s = 0.5 * jnp.tanh(0.5 * pre) + 0.5
    fs = factor * s
    return pre * fs, grad * fs * (1.0 + pre * (1.0 - s))


class Beside:
    def __init__(self, array, got_tx, own_columns, columns):
        channels = columns.shape[2]
        height = columns.shape[1] - PAST
        self.array, self.columns, self.count = array, columns, height // 2
        (before, factor_before), (after, factor_after) = tx_sides(got_tx, height)
        own = own_columns[...].astype(F32)
        lines = (
            before[2 * array],
            before[2 * array + 1],
            own[2 * array],
            own[2 * array + 1],
            after[2 * array],
            after[2 * array + 1],
            jnp.broadcast_to(factor_before, (height, channels)),
            jnp.broadcast_to(factor_after, (height, channels)),
        )
        for n, line in enumerate(lines):
            columns[n, :height] = line
        columns[:, height:] = jnp.zeros((len(lines), PAST, channels), F32)

    def rows(self, n, begin):
        return self.columns[n, pl.ds(begin, self.count, stride=2), :]

    def conv(self, taps6, weights):
        count, channels = self.count, self.columns.shape[2]
        for half in range(2):
            for s in range(2):
                for side in range(2):
                    for e in range(3):
                        at = (3 * s + e) * channels
                        taps6[half, side * count : (side + 1) * count, at : at + channels] = (
                            self.rows(3 * side + e, 2 * half + s).astype(BF16)
                        )
        return deep_product(taps6[0], taps6[1], weights)

    def factor(self, t):
        return jnp.concatenate([self.rows(6, 1 + t), self.rows(7, 1 + t)])


def rims_of(lines, begin, pairs, count):
    return [
        [
            rim_of((None, lines[t, m : m + 1, :]), (lines[t, count + m : count + m + 1, :], None))
            for t in range(2)
        ]
        for m in range(begin, begin + pairs)
    ]


def middle_kernel(kinds_tx, n_dp, x6_in, u6_in, own_columns, factors, *rest):
    got_tx, rest = rest[:kinds_tx], rest[kinds_tx:]
    shards, rest = rest[:n_dp], rest[n_dp:]
    x6, u6, h6, gp2, filters_ref, w_one, w_up, beside_pre = rest[:8]
    columns, beside6, beside_hidden, hidden_rims, edge_cells = rest[8:13]
    pres, grads = rest[13:15], rest[15:17]
    count, breadth, _ = x6.shape
    channels = columns.shape[2]
    mine = shards[0].shape[1]
    me = lax.axis_index("dp")
    for partner, shard in enumerate(shards):
        slot = jnp.bitwise_xor(me, partner)
        filters_ref[:, pl.ds(pl.multiple_of(slot * mine, mine), mine), :] = shard[...]
    pair_weights(w_one, lambda a, e: jnp.transpose(filters_ref[3 * a + e]))
    (before, _), (after, _) = tx_sides(got_tx, 2 * count)
    for array in range(2):
        edge_cells[2 * array] = before[2 * array + 1]
        edge_cells[2 * array + 1] = after[2 * array]
    spot = lax.broadcasted_iota(jnp.int32, (RIM, channels), 0)
    first, last = slice(0, RIM), slice(breadth - RIM, breadth)

    def patch(array, begin, end):
        source, target = ((x6_in, x6), (u6_in, u6))[array]
        for q in range(begin, end):
            for s in range(2):
                i = 2 * q + s
                for e, rows, at in ((0, first, 0), (2, last, RIM - 1)):
                    cell = edge_cells[2 * array + e // 2, i : i + 1, :]
                    lanes = slice((3 * s + e) * channels, (3 * s + e + 1) * channels)
                    value = jnp.where(spot == at, cell, source[q, rows, lanes].astype(F32))
                    target[q, rows, lanes] = value.astype(BF16)

    def convolve(n, at, pairs):
        rows = pairs * breadth
        pres[n % 2][:rows] = pair_conv(x6, w_one, at, pairs)
        grads[n % 2][:rows] = pair_conv(u6, w_up, at, pairs)

    def activate(n, at, pairs):
        rows = pairs * breadth
        here = slice(at, at + pairs)
        for t in range(2):
            lanes = slice(t * channels, (t + 1) * channels)
            hidden, grad_pre = activations(
                pres[n % 2][:rows, lanes],
                grads[n % 2][:rows, lanes],
                factors[here, t].reshape(rows, channels),
            )
            hidden = hidden.reshape(pairs, breadth, channels)
            grad_pre = grad_pre.astype(BF16).reshape(pairs, breadth, channels)
            store_taps(
                h6, here, t, jnp.concatenate([hidden, hidden_rims[here, t]], axis=1), breadth
            )
            gp2[at + t : at + t + pairs, :, (1 - t) * channels : (2 - t) * channels] = grad_pre

    chunks = [(0, 0)]
    while sum(chunks[-1]) < count - 1:
        left = count - 1 - sum(chunks[-1])
        chunks.append((sum(chunks[-1]), min(left, CHUNK, max(3, (left + 1) // 2))))
    del chunks[0]
    done = 0
    for n, (at, pairs) in enumerate(chunks):
        for array in range(2):
            patch(array, done, at + pairs + 1)
        done = at + pairs + 1
        if n == 0:
            pair_weights(w_up, lambda a, e: filters_ref[9 + 3 * (2 - a) + (2 - e)])
        convolve(n, at, pairs)
        if n == 0:
            beside = Beside(0, got_tx, own_columns, columns)
            beside_pre[...] = beside.conv(beside6, w_one)
            for t in range(2):
                lanes = slice(t * channels, (t + 1) * channels)
                beside_hidden[t], _ = activations(beside_pre[:, lanes], 0.0, beside.factor(t))
        for m, rims in enumerate(rims_of(beside_hidden, at, pairs, count)):
            for t in range(2):
                hidden_rims[at + m, t] = rims[t]
        if n > 0:
            activate(n - 1, *chunks[n - 1])
    activate(len(chunks) - 1, *chunks[-1])


def last_kernel(kinds, n_dp, scale, x6, row_edges, edge_factors, up2, h6, gp2, w_one, w_up, *rest):
    kinds_ty, kinds_tx = kinds
    got_tx, rest = rest[:kinds_tx], rest[kinds_tx:]
    got_ty, rest = rest[:kinds_ty], rest[kinds_ty:]
    he, grad_pre_ref, keep_ref, send_ref, xe, ue, sums = rest
    count, breadth, _ = x6.shape
    wide, height = breadth + RIM, 2 * count
    channels = edge_factors.shape[2]
    me = lax.axis_index("dp")

    half = 3 * channels
    taps = 9
    c = channels
    near, far = 2, count - 2

    def flat(value):
        return value.reshape(-1, value.shape[-1])

    def joined(*values):
        return jnp.concatenate(values, axis=1)

    two = outer(
        flat(up2[near:far]), joined(flat(h6[near - 1 : far - 1]), flat(h6[near:far]))
    )
    (before, factor_before), (after, factor_after) = tx_sides(got_tx, height)
    got_rows = sides("ty", [ref[...].astype(F32) for ref in got_ty[::-1]])
    lines = []
    for side, planes in enumerate(got_rows):
        for array, target in enumerate((xe, ue)):
            for s in range(2):
                store_taps(target, 3 * side, s, planes[2 * array + s], wide)
                i = s if side == 0 else height - 2 + s
                rim = rim_of(
                    [before[2 * array + n][i : i + 1] for n in range(2)],
                    [after[2 * array + n][i : i + 1] for n in range(2)],
                )
                own = row_edges[2 * array + side, s].astype(F32)
                store_taps(target, 1 + side, s, jnp.concatenate([own, rim]), wide)
        outer_line = jnp.broadcast_to(planes[4][:, 0:1] + planes[4][:, 1:2], (wide, channels))
        i = 0 if side == 0 else height - 1
        ends = [
            jnp.broadcast_to(column[i : i + 1], (1, channels))
            for column in (factor_before, factor_after)
        ]
        rim = rim_of((None, ends[0]), (ends[1], None))
        inner_line = jnp.concatenate([edge_factors[side], rim])
        lines.append((outer_line, inner_line) if side == 0 else (inner_line, outer_line))

    def edge_conv(lines, weights):
        upper = jnp.concatenate([lines[0], lines[2]])
        lower = jnp.concatenate([lines[1], lines[3]])
        return deep_product(upper, lower, weights)

    pre = edge_conv(xe, w_one)
    grad = edge_conv(ue, w_up)
    one = outer(
        flat(gp2[near:far]),
        joined(
            flat(x6[near - 1 : far - 1, :, half:]),
            flat(x6[near:far]),
            flat(x6[near + 1 : far + 1, :, :half]),
        ),
    )
    inner_grads = []
    for side in range(2):
        rows = slice(side * wide, (side + 1) * wide)
        for t in range(2):
            lanes = slice(t * channels, (t + 1) * channels)
            hidden, grad_pre = activations(pre[rows, lanes], grad[rows, lanes], lines[side][t])
            grad_pre_ref[side, t] = grad_pre.astype(BF16)
            store_taps(he, side, t, hidden, breadth)
            if t != side:
                inner_grads.append(grad_pre[:breadth].astype(BF16))

    def ends(*values):
        return jnp.concatenate([flat(value) for value in values])

    two += outer(
        ends(up2[:near], up2[far:]),
        joined(
            ends(he[0], h6[: near - 1], h6[far - 1 :]),
            ends(h6[:near], h6[far:], he[1]),
        ),
    )
    one += outer(
        ends(
            joined(inner_grads[0], gp2[0, :, c:]),
            gp2[1:near],
            gp2[far : count - 1],
            joined(gp2[count - 1, :, :c], inner_grads[1]),
        ),
        joined(
            ends(xe[0, :breadth, half:], x6[: near - 1, :, half:], x6[far - 1 : count - 1, :, half:]),
            ends(x6[:near], x6[far:]),
            ends(x6[1 : near + 1, :, :half], x6[far + 1 :, :, :half], xe[3, :breadth, :half]),
        ),
    )

    def write(level_at, a, total):
        for e in range(3):
            part = (total[:, e * channels : (e + 1) * channels] * scale).astype(BF16)
            sums[level_at * taps + 3 * a + e] = part

    first, second = two[:, : 2 * half], two[:, 2 * half :]
    write(1, 0, first[:c, :half] + first[c:, half:])
    write(1, 1, first[:c, half:] + second[c:, :half])
    write(1, 2, second[:c, :half] + second[c:, half:])
    first, second, third = one[:, :half], one[:, half : 3 * half], one[:, 3 * half :]
    write(0, 0, first[:c] + second[c:, :half])
    write(0, 1, second[:c, :half] + second[c:, half:])
    write(0, 2, second[:c, half:] + third[c:])
    mine = keep_ref.shape[2]
    for partner in range(n_dp):
        slot = jnp.bitwise_xor(me, partner)
        target = send_ref if partner % 2 else keep_ref
        target[partner // 2] = sums[:, pl.ds(pl.multiple_of(slot * mine, mine), mine), :]


def output_kernel(middle, edges, filters, target, weights):
    count, breadth, _ = middle.shape
    channels = target.shape[3]
    pair_weights(weights, lambda a, e: jnp.transpose(filters[9 + 3 * a + e]))

    def write(result, at, pairs):
        for n in range(pairs):
            for t in range(2):
                target[0, 2 * (at + n) + t] = result[
                    n * breadth : (n + 1) * breadth, t * channels : (t + 1) * channels
                ]

    for at in range(0, count - 1, 2 * CHUNK):
        pairs = min(2 * CHUNK, count - 1 - at)
        write(pair_conv(middle, weights, at, pairs).astype(BF16), at + 1, pairs)
    upper = jnp.concatenate([edges[0], middle[count - 1]])
    lower = jnp.concatenate([middle[0], edges[1]])
    result = deep_product(upper, lower, weights)
    write(result[:breadth].astype(BF16), 0, 1)
    write(result[breadth:].astype(BF16), count, 1)


def grad_taps_kernel(kinds_tx, gp2, edges, filters, beside_pre, w_up, own_columns, *rest):
    got_tx, rest = rest[:kinds_tx], rest[kinds_tx:]
    taps6, weights, columns, beside6, beside_grad = rest
    pairs, breadth, _ = taps6.shape
    channels = columns.shape[2]
    pair_weights(weights, lambda a, e: filters[3 * (2 - a) + (2 - e)])
    beside = Beside(1, got_tx, own_columns, columns)
    grad = beside.conv(beside6, w_up)
    for t in range(2):
        lanes = slice(t * channels, (t + 1) * channels)
        _, beside_grad[t] = activations(beside_pre[:, lanes], grad[:, lanes], beside.factor(t))
    rims = rims_of(beside_grad, 0, pairs - 2, pairs - 1)
    for q in range(pairs - 2):
        for s in range(2):
            line = gp2[q + s, :, (1 - s) * channels : (2 - s) * channels].astype(F32)
            store_taps(taps6, q + 1, s, jnp.concatenate([line, rims[q][s]]), breadth)
    for side, q in enumerate((0, pairs - 1)):
        for s in range(2):
            store_taps(taps6, q, s, edges[side, s].astype(F32), breadth)


def grad_input_kernel(taps6, weights, target):
    pairs, breadth, _ = taps6.shape
    channels = target.shape[3]
    for at in range(0, pairs - 1, 2 * CHUNK):
        many = min(2 * CHUNK, pairs - 1 - at)
        result = pair_conv(taps6, weights, at, many).astype(BF16)
        for n in range(many):
            for t in range(2):
                target[0, 2 * (at + n) + t] = result[
                    n * breadth : (n + 1) * breadth, t * channels : (t + 1) * channels
                ]


def split_kernel(kept, got, own, *others):
    near = lax.axis_index("tx")
    far = 1 - near
    taps = own.shape[0]
    for target, half, at in zip((own,) + others, (near, near, far, far), (0, 1, 0, 1)):
        rows = pl.ds(half * taps, taps)
        target[...] = (kept[at, rows].astype(F32) + got[at, rows].astype(F32)).astype(BF16)


def total_kernel(*refs):
    total = refs[0][...].astype(F32)
    for ref in refs[1:-1]:
        total += ref[...].astype(F32)
    refs[-1][...] = total.astype(BF16)


def halves_kernel(own, by_both, by_x, by_y, one, two):
    first = lax.axis_index("tx") == 0
    near = own[...].astype(F32) + by_y[...].astype(F32)
    far = by_x[...].astype(F32) + by_both[...].astype(F32)
    one[...] = jnp.where(first, near, far)
    two[...] = jnp.where(first, far, near)


def add_kernel(more, kept, got, keep_ref, send_ref):
    for n in range(kept.shape[0]):
        total = (kept[n].astype(F32) + got[n].astype(F32)).astype(BF16)
        if more and n % 2:
            send_ref[n // 2] = total
        else:
            keep_ref[n // 2] = total


def sum_kernel(got, total_ref):
    total = got[0].astype(F32)
    for source in range(1, got.shape[0]):
        total += got[source].astype(F32)
    for copy in range(total_ref.shape[0]):
        total_ref[copy] = total.astype(BF16)


def partners(axis, bit):
    return [(i, i ^ bit) for i in range(lax.axis_size(axis))]


def total_by_swaps(kept, sent, run_between):
    sds = jax.ShapeDtypeStruct
    _, taps, mine, channels = kept.shape
    piece = sds((taps // 2, mine, channels), BF16)

    def total(*pieces):
        return pl.pallas_call(
            total_kernel,
            in_specs=[VMEM] * len(pieces),
            out_specs=VMEM,
            out_shape=piece,
            compiler_params=SMALL,
            name="sum_of_pieces",
        )(*pieces)

    got = lax.ppermute(sent, "dp", partners("dp", 1))
    own, by_y, by_x, by_both = pl.pallas_call(
        split_kernel,
        in_specs=[VMEM] * 2,
        out_specs=[VMEM] * 4,
        out_shape=[piece] * 4,
        compiler_params=SMALL,
        name="sum_on_chip",
    )(kept, got)
    both = [(2 * i + j, 2 * (i ^ 2) + (j ^ 1)) for i in range(4) for j in range(2)]
    got = [
        lax.ppermute(by_both, ("dp", "tx"), both),
        lax.ppermute(by_y, "dp", partners("dp", 2)),
        lax.ppermute(by_x, "tx", partners("tx", 1)),
    ]
    got = run_between(0, own, got)
    own = total(own, *got)
    got = run_between(1, own, [lax.ppermute(own, "ty", partners("ty", 2))])
    own = total(own, *got)
    both = [(2 * i + j, 2 * (i ^ 1) + (j ^ 1)) for i in range(4) for j in range(2)]
    got = [
        lax.ppermute(own, ("ty", "tx"), both),
        lax.ppermute(own, "tx", partners("tx", 1)),
        lax.ppermute(own, "ty", partners("ty", 1)),
    ]
    got = run_between(2, own, got)
    return pl.pallas_call(
        halves_kernel,
        in_specs=[VMEM] * 4,
        out_specs=[VMEM] * 2,
        out_shape=[sds(piece.shape, F32)] * 2,
        compiler_params=SMALL,
        name="both_halves",
    )(own, *got)


def total_by_groups(kept, sent, run_between):
    sds = jax.ShapeDtypeStruct
    _, taps, mine, channels = kept.shape
    n_dp = lax.axis_size("dp")
    bit = 1
    while bit < n_dp:
        got = lax.ppermute(sent, "dp", partners("dp", bit))
        half = kept.shape[0] // 2
        bit *= 2
        kept, sent = pl.pallas_call(
            functools.partial(add_kernel, bit < n_dp),
            in_specs=[VMEM] * 2,
            out_specs=[VMEM] * 2,
            out_shape=[sds((max(half, 1),) + kept.shape[1:], BF16)] * 2,
            compiler_params=SMALL,
            name="sum_of_crops",
        )(kept, got)
    tiles = lax.axis_size("ty") * lax.axis_size("tx")
    rows = taps * mine // tiles
    got = lax.all_to_all(kept.reshape(tiles, rows, channels), ("ty", "tx"), 0, 0, tiled=True)
    shared = pl.pallas_call(
        sum_kernel,
        in_specs=[VMEM],
        out_specs=VMEM,
        out_shape=sds((tiles, rows, channels), BF16),
        compiler_params=SMALL,
        name="sum_of_tiles",
    )(got)
    (total,) = run_between(0, shared, [lax.all_to_all(shared, ("ty", "tx"), 0, 0, tiled=True)])
    run_between(1, shared, [total])
    run_between(2, shared, [total])
    total = total.astype(F32).reshape(2, taps // 2, mine, channels)
    return total[0], total[1]


def on_device(features, filter_one, filter_two, speedup, land_mask, offsets, upstream):
    _, height, breadth, channels = features.shape
    mine = filter_one.shape[3]
    n_dp, n_ty, n_tx = (lax.axis_size(axis) for axis in ("dp", "ty", "tx"))
    kinds = kinds_ty, kinds_tx = min(2, n_ty - 1), min(2, n_tx - 1)
    taps = 9
    wide = breadth + RIM
    pairs = height // 2 + 1
    sds = jax.ShapeDtypeStruct

    one, two = (f.reshape(taps, channels, mine).transpose(0, 2, 1) for f in (filter_one, filter_two))
    *tx_sent, factor, shard, own_columns = pl.pallas_call(
        functools.partial(columns_kernel, kinds_tx),
        in_specs=[HBM] * 7,
        out_specs=[VMEM] * (kinds_tx + 3),
        out_shape=[pltpu.VMEM((4 * height + RIM, channels), BF16)] * kinds_tx
        + [pltpu.VMEM((height, breadth), F32), pltpu.VMEM((2 * taps, mine, channels), BF16)]
        + [pltpu.VMEM((4, height, channels), BF16)],
        scratch_shapes=[
            pltpu.VMEM((height * RIM, channels), F32),
            pltpu.VMEM((4, height, RIM, channels), BF16),
            pltpu.VMEM(speedup.shape, F32),
            pltpu.VMEM(land_mask.shape, jnp.int32),
            pltpu.SMEM(offsets.shape, jnp.int32),
            pltpu.SemaphoreType.DMA((9,)),
        ],
        compiler_params=SMALL,
        name="edge_columns",
    )(*in_hbm(offsets, features, upstream, speedup, land_mask, one, two))
    tx_got = swaps("tx", tx_sent)
    shards = [shard] + [
        lax.ppermute(shard, "dp", partners("dp", partner)) for partner in range(1, n_dp)
    ]

    count = height // 2
    k6 = 6 * channels
    x6, u6, up2, factors, edge_factors, row_edges = pl.pallas_call(
        own_kernel,
        in_specs=[HBM] * 2 + [VMEM],
        out_specs=[VMEM] * 6,
        out_shape=[
            pltpu.VMEM((count, breadth, k6), BF16),
            pltpu.VMEM((count, breadth, k6), BF16),
            pltpu.VMEM((count, breadth, 2 * channels), BF16),
            pltpu.VMEM((count - 1, 2, breadth, channels), F32),
            pltpu.VMEM((2, breadth, channels), F32),
            pltpu.VMEM((4, 2, breadth, channels), BF16),
        ],
        scratch_shapes=[
            pltpu.VMEM((2, height, breadth, channels), BF16),
            pltpu.SemaphoreType.DMA((2, 4)),
        ],
        compiler_params=SMALL,
        cost_estimate=pl.CostEstimate(flops=100000, bytes_accessed=100000, transcendentals=0),
        name="own_column_taps",
    )(*in_hbm(features, upstream), factor)
    row_edges, tx_got = lax.optimization_barrier((row_edges, tx_got))
    ty_sent = pl.pallas_call(
        functools.partial(rows_kernel, kinds_tx),
        in_specs=[VMEM] * (2 + kinds_tx),
        out_specs=[VMEM] * kinds_ty,
        out_shape=[pltpu.VMEM((PLANES, wide, channels), BF16)] * kinds_ty,
        compiler_params=SMALL,
        cost_estimate=pl.CostEstimate(flops=100000000000, bytes_accessed=100000000, transcendentals=0),
        name="edge_rows",
    )(row_edges, factor, *tx_got)
    ty_got = swaps("ty", ty_sent)

    weights = pltpu.VMEM((2, k6, 2 * channels), BF16)
    rows = CHUNK * breadth
    beside_scratch = [
        pltpu.VMEM((8, height + PAST, channels), F32),
        pltpu.VMEM((2, 2 * count, k6), BF16),
        pltpu.VMEM((2, 2 * count, channels), F32),
    ]
    x6, u6, h6, gp2, filters, w_one, w_up, beside_pre = pl.pallas_call(
        functools.partial(middle_kernel, kinds_tx, n_dp),
        in_specs=[VMEM] * (4 + kinds_tx + n_dp),
        out_specs=[VMEM] * 8,
        out_shape=[
            pltpu.VMEM(x6.shape, BF16),
            pltpu.VMEM(u6.shape, BF16),
            pltpu.VMEM((count - 1, breadth, k6), BF16),
            pltpu.VMEM((count, breadth, 2 * channels), BF16),
            pltpu.VMEM((2 * taps, channels, channels), BF16),
            weights,
            weights,
            pltpu.VMEM((2 * count, 2 * channels), F32),
        ],
        input_output_aliases={0: 0, 1: 1},
        scratch_shapes=beside_scratch
        + [
            pltpu.VMEM((count - 1, 2, RIM, channels), F32),
            pltpu.VMEM((4, height, channels), F32),
        ]
        + [pltpu.VMEM((rows, 2 * channels), F32)] * 4,
        compiler_params=pltpu.CompilerParams(vmem_limit_bytes=20 * MIB),
        cost_estimate=pl.CostEstimate(
            flops=2 * 18 * height * breadth * channels * channels,
            bytes_accessed=20 * MIB,
            transcendentals=height * breadth * channels,
        ),
        name="middle_rows",
    )(x6, u6, own_columns, factors, *tx_got, *shards)

    scale = 1.0 / math.sqrt(height * breadth * n_dp * n_ty * n_tx)
    h6_edges, grad_pre_edges, kept, sent = pl.pallas_call(
        functools.partial(last_kernel, kinds, n_dp, scale),
        in_specs=[VMEM] * (8 + kinds_tx + kinds_ty),
        out_specs=[VMEM] * 4,
        out_shape=[
            pltpu.VMEM((2, breadth, k6), BF16),
            pltpu.VMEM((2, 2, wide, channels), BF16),
            pltpu.VMEM((n_dp // 2, 2 * taps, mine, channels), BF16),
            pltpu.VMEM((n_dp // 2, 2 * taps, mine, channels), BF16),
        ],
        scratch_shapes=[
            pltpu.VMEM((4, wide, k6), BF16),
            pltpu.VMEM((4, wide, k6), BF16),
            pltpu.VMEM((2 * taps, channels, channels), BF16),
        ],
        compiler_params=pltpu.CompilerParams(vmem_limit_bytes=20 * MIB),
        name="outer_rows_and_filter_grads",
    )(x6, row_edges, edge_factors, up2, h6, gp2, w_one, w_up, *tx_got, *ty_got[::-1])

    def conv_cost(macs):
        return pl.CostEstimate(
            flops=18 * macs * height * breadth * channels * channels,
            bytes_accessed=4 * height * breadth * channels,
            transcendentals=0,
        )

    def output_step(ready):
        h6_now, _ = lax.optimization_barrier((h6_edges, ready))
        return pl.pallas_call(
            output_kernel,
            in_specs=[VMEM] * 3,
            out_specs=VMEM,
            out_shape=sds(features.shape, BF16),
            scratch_shapes=[weights],
            compiler_params=MEDIUM,
            cost_estimate=conv_cost(1),
            name="output",
        )(h6, h6_now, filters)

    def taps_step(ready):
        edges, _ = lax.optimization_barrier((grad_pre_edges, ready))
        return pl.pallas_call(
            functools.partial(grad_taps_kernel, kinds_tx),
            in_specs=[VMEM] * (6 + kinds_tx),
            out_specs=[VMEM] * 2,
            out_shape=[pltpu.VMEM((pairs, breadth, k6), BF16), weights],
            scratch_shapes=beside_scratch,
            compiler_params=MEDIUM,
            cost_estimate=conv_cost(0),
            name="grad_pre_taps",
        )(gp2, edges, filters, beside_pre, w_up, own_columns, *tx_got)

    def grad_input_step(ready):
        g6, w_back = results.pop()
        g6, _ = lax.optimization_barrier((g6, ready))
        return pl.pallas_call(
            grad_input_kernel,
            in_specs=[VMEM] * 2,
            out_specs=VMEM,
            out_shape=sds(features.shape, BF16),
            compiler_params=MEDIUM,
            cost_estimate=conv_cost(1),
            name="grad_input",
        )(g6, w_back)

    results = []

    def run_between(which, ready, got):
        result = (output_step, taps_step, grad_input_step)[which](ready)
        result, got = lax.optimization_barrier((result, got))
        results.append(result)
        return got

    if (n_dp, n_ty, n_tx) == (4, 4, 2):
        grads = total_by_swaps(kept, sent, run_between)
    else:
        grads = total_by_groups(kept, sent, run_between)
    grads = [g.reshape(3, 3, mine, channels).transpose(0, 1, 3, 2) for g in grads]
    return results[0], results[1], grads[0], grads[1]


def solution(mesh):
    in_specs = (
        P("dp", "ty", "tx", None),
        P(None, None, None, "dp"),
        P(None, None, None, "dp"),
        P("dp", "ty", "tx"),
        P("dp", "ty", "tx"),
        P("dp", None),
        P("dp", "ty", "tx", None),
    )
    out_specs = (
        P("dp", "ty", "tx", None),
        P("dp", "ty", "tx", None),
        P(None, None, None, "dp"),
        P(None, None, None, "dp"),
    )
    return jax.shard_map(
        on_device, mesh=mesh, in_specs=in_specs, out_specs=out_specs, check_vma=False
    )
```

profile of v0, /device:TPU:0, one launch (start us, length us, event | category | flops | bytes accessed | tf_op | source)
XLA Modules:
  0.0 46.2 jit_solution(5175619378143707249)
XLA Ops:
  0.6 1.4 %edge_columns.1 = (bf16[272,128]{1,0:T(8,128)(2,1)S(1)}, f32[64,64]{1,0:T(8,128)S(1)}, bf16[18,32,128]{2,1,0:T(8,128)(2,1)S(1)}, bf16[4,64,128]{2,1,0:T(8,128)(2,1)S(1)}) custom-call(s32[1,2]{1,0:T(1,128)} %offsets.1, bf16[1,64,64,128]{3,2,1,0:T(8,128)(2,1)} %features.3, bf16[1,64,64,128]{3,2,1,0:T(8,128)(2,1)} %upstream.3, f32[1,64,64]{2,1,0:T(8,128)} %speedup.1, ...), custom_call_target="tpu_custom_call" | custom-call | tf_op jit(solution)/shard_map/edge_columns/pallas_call | solution.py:715
  2.1 3.0 %collective-permute-start = (bf16[272,128]{1,0:T(8,128)(2,1)S(1)}, bf16[272,128]{1,0:T(8,128)(2,1)S(1)}, u32[]{:S(2)}, u32[]{:S(2)}) collective-permute-start(bf16[272,128]{1,0:T(8,128)(2,1)S(1)} %get-tuple-element.57), channel_id=1, source_target_pairs={{0,1},{1,0},{2,3},{3,2},{4,5},{5,4},{6,7},{7,6},{8,9},{9,8},{10,11... | collective-permute-start | bytes 208904 | tf_op jit(solution)/shard_map/ppermute | solution.py:40
  5.1 0.0 collective-permute-start.1
  5.1 1.5 %collective-permute-start.2 = (bf16[18,32,128]{2,1,0:T(8,128)(2,1)S(1)}, bf16[18,32,128]{2,1,0:T(8,128)(2,1)S(1)}, u32[]{:S(2)}, u32[]{:S(2)}) collective-permute-start(bf16[18,32,128]{2,1,0:T(8,128)(2,1)S(1)} %get-tuple-element.59.rest_1_), channel_id=1, source_target_pairs={{0,16},{8,24},{16,0},{24,8},{1,17},{9,25},{17,1},{25,9},{2,18},{10... | collective-permute-start | bytes 442376 | tf_op jit(solution)/shard_map/ppermute | solution.py:735
  6.6 0.3 collective-permute-start.3
  6.9 2.3 %own_column_taps.1 = (bf16[32,64,768]{2,1,0:T(8,128)(2,1)S(1)}, bf16[32,64,768]{2,1,0:T(8,128)(2,1)S(1)}, bf16[32,64,256]{2,1,0:T(8,128)(2,1)S(1)}, f32[31,2,64,...) custom-call(bf16[1,64,64,128]{3,2,1,0:T(8,128)(2,1)} %features.3, ...), custom_call_target="tpu_custom_call" | custom-call | flops 100000 | bytes 100000 | tf_op jit(solution)/shard_map/own_column_taps/pallas_call | solution.py:740
  9.3 0.0 collective-permute-done.rest_0_
  9.3 0.2 edge_rows.1
  9.5 0.7 %collective-permute-start.4 = (bf16[5,80,128]{2,1,0:T(8,128)(2,1)S(1)}, bf16[5,80,128]{2,1,0:T(8,128)(2,1)S(1)}, u32[]{:S(2)}, u32[]{:S(2)}) collective-permute-start(bf16[5,80,128]{2,1,0:T(8,128)(2,1)S(1)} %get-tuple-element.68), channel_id=1, source_target_pairs={{2,4},{4,2},{3,5},{5,3},{10,12},{12,10},{11,13},{13,11},{18,20},{2... | collective-permute-start | bytes 307208 | tf_op jit(solution)/shard_map/ppermute | solution.py:40
  10.2 4.5 %collective-permute-start.5 = (bf16[5,80,128]{2,1,0:T(8,128)(2,1)S(1)}, bf16[5,80,128]{2,1,0:T(8,128)(2,1)S(1)}, u32[]{:S(2)}, u32[]{:S(2)}) collective-permute-start(bf16[5,80,128]{2,1,0:T(8,128)(2,1)S(1)} %get-tuple-element.69), channel_id=1, source_target_pairs={{0,2},{2,0},{4,6},{6,4},{1,3},{3,1},{5,7},{7,5},{8,10},{10,8},{12,... | collective-permute-start | bytes 307208 | tf_op jit(solution)/shard_map/ppermute | solution.py:40
  14.7 0.0 collective-permute-done.1.rest_2_
  14.7 0.0 collective-permute-done.2.rest_3_
  14.7 0.0 collective-permute-done.3.rest_4_
  14.7 4.9 %middle_rows.1 = (bf16[32,64,768]{2,1,0:T(8,128)(2,1)S(1)}, bf16[32,64,768]{2,1,0:T(8,128)(2,1)S(1)}, bf16[31,64,768]{2,1,0:T(8,128)(2,1)S(1)}, bf16[32,64,256]{...) custom-call(bf16[32,64,768]{2,1,0:T(8,128)(2,1)S(1)} %get-tuple-elem, ...), custom_call_target="tpu_custom_call", output_to_operand_aliasing={{0}: (0, {}), {1}: (1, {})} | custom-call | flops 2415919104 | bytes 20971520 | tf_op jit(solution)/shard_map/middle_rows/pallas_call | solution.py:779
  19.6 0.0 collective-permute-done.4.rest_1_
  19.6 0.0 collective-permute-done.5.rest_2_
  19.6 4.1 %outer_rows_and_filter_grads.1 = (bf16[2,64,768]{2,1,0:T(8,128)(2,1)S(1)}, bf16[2,2,80,128]{3,2,1,0:T(8,128)(2,1)S(1)}, bf16[2,18,32,128]{3,2,1,0:T(8,128)(2,1)S(1)}, bf16[2,18,32,128]{3,2,1,0:T(8,128)(2,1)S(1)}) custom-call(bf16[32,64,768]{2,1,0:T(8,128)(2,1)S(1)} %get-tuple-element.61.x6, bf16[4,2,64,128]{3,2,1,0:T(8,128)(2,1)S(1)} %get-tuple-element.62.edges.row_edges, ...), custom_call_target="tpu_custom_call" | custom-call | tf_op jit(solution)/shard_map/outer_rows_and_filter_grads/pallas_call | solution.py:810
  23.7 0.1 collective-permute-start.6
  23.8 1.6 %collective-permute-done.6.got = bf16[2,18,32,128]{3,2,1,0:T(8,128)(2,1)S(1)} collective-permute-done((bf16[2,18,32,128]{3,2,1,0:T(8,128)(2,1)S(1)}, bf16[2,18,32,128]{3,2,1,0:T(8,128)(2,1)S(1)}, u32[]{:S(2)}, u32[]{:S(2)}) %collective-permute-start.6) | collective-permute-done | bytes 294944 | tf_op jit(solution)/shard_map/ppermute | solution.py:633
  25.3 0.1 sum_on_chip.1
  25.4 1.6 %collective-permute-start.7 = (bf16[9,32,128]{2,1,0:T(8,128)(2,1)S(1)}, bf16[9,32,128]{2,1,0:T(8,128)(2,1)S(1)}, u32[]{:S(2)}, u32[]{:S(2)}) collective-permute-start(bf16[9,32,128]{2,1,0:T(8,128)(2,1)S(1)} %get-tuple-element.76), channel_id=1, source_target_pairs={{0,17},{1,16},{8,25},{9,24},{16,1},{17,0},{24,9},{25,8},{2,19},{3,... | collective-permute-start | bytes 221192 | tf_op jit(solution)/shard_map/ppermute | solution.py:644
  27.0 0.5 %collective-permute-start.8 = (bf16[9,32,128]{2,1,0:T(8,128)(2,1)S(1)}, bf16[9,32,128]{2,1,0:T(8,128)(2,1)S(1)}, u32[]{:S(2)}, u32[]{:S(2)}) collective-permute-start(bf16[9,32,128]{2,1,0:T(8,128)(2,1)S(1)} %get-tuple-element.77), channel_id=1, source_target_pairs={{0,16},{8,24},{16,0},{24,8},{1,17},{9,25},{17,1},{25,9},{2,18},{10... | collective-permute-start | bytes 221192 | tf_op jit(solution)/shard_map/ppermute | solution.py:645
  27.5 1.5 %collective-permute-start.9 = (bf16[9,32,128]{2,1,0:T(8,128)(2,1)S(1)}, bf16[9,32,128]{2,1,0:T(8,128)(2,1)S(1)}, u32[]{:S(2)}, u32[]{:S(2)}) collective-permute-start(bf16[9,32,128]{2,1,0:T(8,128)(2,1)S(1)} %get-tuple-element.78), channel_id=1, source_target_pairs={{0,1},{1,0},{2,3},{3,2},{4,5},{5,4},{6,7},{7,6},{8,9},{9,8},{10,11... | collective-permute-start | bytes 221192 | tf_op jit(solution)/shard_map/ppermute | solution.py:646
  29.0 3.0 %output.1 = bf16[1,64,64,128]{3,2,1,0:T(8,128)(2,1)} custom-call(bf16[31,64,768]{2,1,0:T(8,128)(2,1)S(1)} %get-tuple-element.60.h6.middle, bf16[2,64,768]{2,1,0:T(8,128)(2,1)S(1)} %get-tuple-element.74.edges, bf16[18,128,128]{2,1,0:T(8,128)(2,1)S(1)} %get-tuple-element.75.filters), custom_call_target="tpu_custom_call" | custom-call | flops 1207959552 | bytes 2097152 | tf_op jit(solution)/shard_map/output/pallas_call | solution.py:838
  32.0 0.0 collective-permute-done.7.refs_1_
  32.0 0.3 collective-permute-done.8.refs_2_
  32.3 0.1 collective-permute-done.9.refs_3_
  32.4 2.2 %collective-permute-start.10 = (bf16[9,32,128]{2,1,0:T(8,128)(2,1)S(1)}, bf16[9,32,128]{2,1,0:T(8,128)(2,1)S(1)}, u32[]{:S(2)}, u32[]{:S(2)}) collective-permute-start(bf16[9,32,128]{2,1,0:T(8,128)(2,1)S(1)} %sum_of_pieces.2.refs_0_), channel_id=1, source_target_pairs={{0,4},{2,6},{4,0},{6,2},{1,5},{3,7},{5,1},{7,3},{8,12},{10,14},{12... | collective-permute-start | bytes 221192 | tf_op jit(solution)/shard_map/ppermute | solution.py:650
  34.6 1.0 %grad_pre_taps.1 = (bf16[33,64,768]{2,1,0:T(8,128)(2,1)S(1)}, bf16[2,768,256]{2,1,0:T(8,128)(2,1)S(1)}) custom-call(bf16[32,64,256]{2,1,0:T(8,128)(2,1)S(1)} %get-tuple-element.65.gp2, bf16[2,2,80,128]{3,2,1,0:T(8,128)(2,1)S(1)} %get-tuple-element.84.edges, bf16[18,128,128]{2,1,0:T(8,128)(2,1)S(1)} %get-tuple-element.75.filters, ...), custom_call_target="tpu_custom_call" | custom-call | bytes 2097152 | tf_op jit(solution)/shard_map/grad_pre_taps/pallas_call | solution.py:851
  35.5 3.5 %collective-permute-done.10.refs_1_ = bf16[9,32,128]{2,1,0:T(8,128)(2,1)S(1)} collective-permute-done((bf16[9,32,128]{2,1,0:T(8,128)(2,1)S(1)}, bf16[9,32,128]{2,1,0:T(8,128)(2,1)S(1)}, u32[]{:S(2)}, u32[]{:S(2)}) %collective-permute-start.10) | collective-permute-done | bytes 73760 | tf_op jit(solution)/shard_map/ppermute | solution.py:650
  39.1 0.2 collective-permute-start.11
  39.3 1.5 %collective-permute-start.12 = (bf16[9,32,128]{2,1,0:T(8,128)(2,1)S(1)}, bf16[9,32,128]{2,1,0:T(8,128)(2,1)S(1)}, u32[]{:S(2)}, u32[]{:S(2)}) collective-permute-start(bf16[9,32,128]{2,1,0:T(8,128)(2,1)S(1)} %sum_of_pieces.3.own), channel_id=1, source_target_pairs={{0,1},{1,0},{2,3},{3,2},{4,5},{5,4},{6,7},{7,6},{8,9},{9,8},{10,11... | collective-permute-start | bytes 221192 | tf_op jit(solution)/shard_map/ppermute | solution.py:655
  40.8 1.9 %collective-permute-start.13 = (bf16[9,32,128]{2,1,0:T(8,128)(2,1)S(1)}, bf16[9,32,128]{2,1,0:T(8,128)(2,1)S(1)}, u32[]{:S(2)}, u32[]{:S(2)}) collective-permute-start(bf16[9,32,128]{2,1,0:T(8,128)(2,1)S(1)} %sum_of_pieces.3.own), channel_id=1, source_target_pairs={{0,2},{2,0},{4,6},{6,4},{1,3},{3,1},{5,7},{7,5},{8,10},{10,8},{12,... | collective-permute-start | bytes 221192 | tf_op jit(solution)/shard_map/ppermute | solution.py:656
  42.6 2.8 %grad_input.1 = bf16[1,64,64,128]{3,2,1,0:T(8,128)(2,1)} custom-call(bf16[33,64,768]{2,1,0:T(8,128)(2,1)S(1)} %get-tuple-element.90.taps6, bf16[2,768,256]{2,1,0:T(8,128)(2,1)S(1)} %get-tuple-element.91.weights), custom_call_target="tpu_custom_call" | custom-call | flops 1207959552 | bytes 2097152 | tf_op jit(solution)/shard_map/grad_input/pallas_call | solution.py:865
  45.4 0.0 collective-permute-done.11.by_both
  45.4 0.0 collective-permute-done.12.by_x
  45.4 0.0 collective-permute-done.13.by_y
  45.4 0.8 %both_halves.1 = (f32[9,32,128]{2,1,0:T(8,128)}, f32[9,32,128]{2,1,0:T(8,128)}) custom-call(bf16[9,32,128]{2,1,0:T(8,128)(2,1)S(1)} %sum_of_pieces.3.own, bf16[9,32,128]{2,1,0:T(8,128)(2,1)S(1)} %collective-permute-done.11.by_both, bf16[9,32,128]{2,1,0:T(8,128)(2,1)S(1)} %collective-permute-done.12.by_x, bf16[9,32,128]{2,1,0:T(8,128)(2,1)S(1)} %collective-permute-done.13.by_y), custom_call_target="tpu_custom_call" | custom-call | tf_op jit(solution)/shard_map/both_halves/pallas_call | solution.py:659
  (2 shorter events, 0.1 us)
Async XLA Ops:
  2.1 7.2 %collective-permute-start = (bf16[272,128]{1,0:T(8,128)(2,1)S(1)}, bf16[272,128]{1,0:T(8,128)(2,1)S(1)}, u32[]{:S(2)}, u32[]{:S(2)}) collective-permute-start(bf16[272,128]{1,0:T(8,128)(2,1)S(1)} %get-tuple-element.57), channel_id=1, source_target_pairs={{0,1},{1,0},{2,3},{3,2},{4,5},{5,4},{6,7},{7,6},{8,9},{9,8},{10,11... | collective-permute-start | bytes 208904 | tf_op jit(solution)/shard_map/ppermute | solution.py:40
  5.1 9.6 %collective-permute-start.1 = (bf16[18,32,128]{2,1,0:T(8,128)(2,1)S(1)}, bf16[18,32,128]{2,1,0:T(8,128)(2,1)S(1)}, u32[]{:S(2)}, u32[]{:S(2)}) collective-permute-start(bf16[18,32,128]{2,1,0:T(8,128)(2,1)S(1)} %get-tuple-element.59.rest_1_), channel_id=1, source_target_pairs={{0,8},{8,0},{16,24},{24,16},{1,9},{9,1},{17,25},{25,17},{2,10},{10... | collective-permute-start | bytes 442376 | tf_op jit(solution)/shard_map/ppermute | solution.py:735
  5.1 9.6 %collective-permute-start.2 = (bf16[18,32,128]{2,1,0:T(8,128)(2,1)S(1)}, bf16[18,32,128]{2,1,0:T(8,128)(2,1)S(1)}, u32[]{:S(2)}, u32[]{:S(2)}) collective-permute-start(bf16[18,32,128]{2,1,0:T(8,128)(2,1)S(1)} %get-tuple-element.59.rest_1_), channel_id=1, source_target_pairs={{0,16},{8,24},{16,0},{24,8},{1,17},{9,25},{17,1},{25,9},{2,18},{10... | collective-permute-start | bytes 442376 | tf_op jit(solution)/shard_map/ppermute | solution.py:735
  6.6 8.1 %collective-permute-start.3 = (bf16[18,32,128]{2,1,0:T(8,128)(2,1)S(1)}, bf16[18,32,128]{2,1,0:T(8,128)(2,1)S(1)}, u32[]{:S(2)}, u32[]{:S(2)}) collective-permute-start(bf16[18,32,128]{2,1,0:T(8,128)(2,1)S(1)} %get-tuple-element.59.rest_1_), channel_id=1, source_target_pairs={{0,24},{8,16},{16,8},{24,0},{1,25},{9,17},{17,9},{25,1},{2,26},{10... | collective-permute-start | bytes 442376 | tf_op jit(solution)/shard_map/ppermute | solution.py:735
  9.5 10.0 %collective-permute-start.4 = (bf16[5,80,128]{2,1,0:T(8,128)(2,1)S(1)}, bf16[5,80,128]{2,1,0:T(8,128)(2,1)S(1)}, u32[]{:S(2)}, u32[]{:S(2)}) collective-permute-start(bf16[5,80,128]{2,1,0:T(8,128)(2,1)S(1)} %get-tuple-element.68), channel_id=1, source_target_pairs={{2,4},{4,2},{3,5},{5,3},{10,12},{12,10},{11,13},{13,11},{18,20},{2... | collective-permute-start | bytes 307208 | tf_op jit(solution)/shard_map/ppermute | solution.py:40
  10.2 9.4 %collective-permute-start.5 = (bf16[5,80,128]{2,1,0:T(8,128)(2,1)S(1)}, bf16[5,80,128]{2,1,0:T(8,128)(2,1)S(1)}, u32[]{:S(2)}, u32[]{:S(2)}) collective-permute-start(bf16[5,80,128]{2,1,0:T(8,128)(2,1)S(1)} %get-tuple-element.69), channel_id=1, source_target_pairs={{0,2},{2,0},{4,6},{6,4},{1,3},{3,1},{5,7},{7,5},{8,10},{10,8},{12,... | collective-permute-start | bytes 307208 | tf_op jit(solution)/shard_map/ppermute | solution.py:40
  23.7 1.6 %collective-permute-start.6 = (bf16[2,18,32,128]{3,2,1,0:T(8,128)(2,1)S(1)}, bf16[2,18,32,128]{3,2,1,0:T(8,128)(2,1)S(1)}, u32[]{:S(2)}, u32[]{:S(2)}) collective-permute-start(bf16[2,18,32,128]{3,2,1,0:T(8,128)(2,1)S(1)} %get-tuple-element.72), channel_id=1, source_target_pairs={{0,8},{8,0},{16,24},{24,16},{1,9},{9,1},{17,25},{25,17},{2,10},{10... | collective-permute-start | bytes 884744 | tf_op jit(solution)/shard_map/ppermute | solution.py:633
  25.4 6.6 %collective-permute-start.7 = (bf16[9,32,128]{2,1,0:T(8,128)(2,1)S(1)}, bf16[9,32,128]{2,1,0:T(8,128)(2,1)S(1)}, u32[]{:S(2)}, u32[]{:S(2)}) collective-permute-start(bf16[9,32,128]{2,1,0:T(8,128)(2,1)S(1)} %get-tuple-element.76), channel_id=1, source_target_pairs={{0,17},{1,16},{8,25},{9,24},{16,1},{17,0},{24,9},{25,8},{2,19},{3,... | collective-permute-start | bytes 221192 | tf_op jit(solution)/shard_map/ppermute | solution.py:644
  27.0 5.3 %collective-permute-start.8 = (bf16[9,32,128]{2,1,0:T(8,128)(2,1)S(1)}, bf16[9,32,128]{2,1,0:T(8,128)(2,1)S(1)}, u32[]{:S(2)}, u32[]{:S(2)}) collective-permute-start(bf16[9,32,128]{2,1,0:T(8,128)(2,1)S(1)} %get-tuple-element.77), channel_id=1, source_target_pairs={{0,16},{8,24},{16,0},{24,8},{1,17},{9,25},{17,1},{25,9},{2,18},{10... | collective-permute-start | bytes 221192 | tf_op jit(solution)/shard_map/ppermute | solution.py:645
  27.5 4.8 %collective-permute-start.9 = (bf16[9,32,128]{2,1,0:T(8,128)(2,1)S(1)}, bf16[9,32,128]{2,1,0:T(8,128)(2,1)S(1)}, u32[]{:S(2)}, u32[]{:S(2)}) collective-permute-start(bf16[9,32,128]{2,1,0:T(8,128)(2,1)S(1)} %get-tuple-element.78), channel_id=1, source_target_pairs={{0,1},{1,0},{2,3},{3,2},{4,5},{5,4},{6,7},{7,6},{8,9},{9,8},{10,11... | collective-permute-start | bytes 221192 | tf_op jit(solution)/shard_map/ppermute | solution.py:646
  32.4 6.7 %collective-permute-start.10 = (bf16[9,32,128]{2,1,0:T(8,128)(2,1)S(1)}, bf16[9,32,128]{2,1,0:T(8,128)(2,1)S(1)}, u32[]{:S(2)}, u32[]{:S(2)}) collective-permute-start(bf16[9,32,128]{2,1,0:T(8,128)(2,1)S(1)} %sum_of_pieces.2.refs_0_), channel_id=1, source_target_pairs={{0,4},{2,6},{4,0},{6,2},{1,5},{3,7},{5,1},{7,3},{8,12},{10,14},{12... | collective-permute-start | bytes 221192 | tf_op jit(solution)/shard_map/ppermute | solution.py:650
  39.1 6.3 %collective-permute-start.11 = (bf16[9,32,128]{2,1,0:T(8,128)(2,1)S(1)}, bf16[9,32,128]{2,1,0:T(8,128)(2,1)S(1)}, u32[]{:S(2)}, u32[]{:S(2)}) collective-permute-start(bf16[9,32,128]{2,1,0:T(8,128)(2,1)S(1)} %sum_of_pieces.3.own), channel_id=1, source_target_pairs={{0,3},{1,2},{2,1},{3,0},{4,7},{5,6},{6,5},{7,4},{8,11},{9,10},{10,... | collective-permute-start | bytes 221192 | tf_op jit(solution)/shard_map/ppermute | solution.py:654
  39.3 6.1 %collective-permute-start.12 = (bf16[9,32,128]{2,1,0:T(8,128)(2,1)S(1)}, bf16[9,32,128]{2,1,0:T(8,128)(2,1)S(1)}, u32[]{:S(2)}, u32[]{:S(2)}) collective-permute-start(bf16[9,32,128]{2,1,0:T(8,128)(2,1)S(1)} %sum_of_pieces.3.own), channel_id=1, source_target_pairs={{0,1},{1,0},{2,3},{3,2},{4,5},{5,4},{6,7},{7,6},{8,9},{9,8},{10,11... | collective-permute-start | bytes 221192 | tf_op jit(solution)/shard_map/ppermute | solution.py:655
  40.8 4.6 %collective-permute-start.13 = (bf16[9,32,128]{2,1,0:T(8,128)(2,1)S(1)}, bf16[9,32,128]{2,1,0:T(8,128)(2,1)S(1)}, u32[]{:S(2)}, u32[]{:S(2)}) collective-permute-start(bf16[9,32,128]{2,1,0:T(8,128)(2,1)S(1)} %sum_of_pieces.3.own), channel_id=1, source_target_pairs={{0,2},{2,0},{4,6},{6,4},{1,3},{3,1},{5,7},{7,5},{8,10},{10,8},{12,... | collective-permute-start | bytes 221192 | tf_op jit(solution)/shard_map/ppermute | solution.py:656
where the time goes:
time: 46.4 us; the launch traced here: 46.2 us
  Pallas kernels  20.6 us (44%)
  starting transfers between devices  19.3 us (42%)
  waiting for transfers between devices  5.45 us (12%)
  between operations  0.74 us (2%)
    ppermute x3, starting transfers between devices, swaps(): got.append(lax.ppermute(sent[kind], axis, pairs))  8.13 us
    pallas_call x1, Pallas kernels, on_device(): pl.pallas_call(functools.partial(middle_kernel, kinds_tx, n_dp), in_specs...  4.89 us
    pallas_call x1, Pallas kernels, on_device(): pl.pallas_call(functools.partial(last_kernel, kinds, n_dp, scale), in_spe...  4.1 us
    ppermute x1, waiting for transfers between devices, total_by_swaps(): got = run_between(1, own, [lax.ppermute(own, 'ty', partners('ty', 2))])  3.52 us
    pallas_call x1, Pallas kernels, output_step(): pl.pallas_call(output_kernel, in_specs=[VMEM] * 3, out_specs=VMEM, out_sh...  3.01 us
    pallas_call x1, Pallas kernels, grad_input_step(): pl.pallas_call(grad_input_kernel, in_specs=[VMEM] * 2, out_specs=VMEM, ou...  2.78 us
    pallas_call x1, Pallas kernels, on_device(): pl.pallas_call(own_kernel, in_specs=[HBM] * 2 + [VMEM], out_specs=[VMEM]...  2.32 us
    ppermute x1, starting transfers between devices, total_by_swaps(): got = run_between(1, own, [lax.ppermute(own, 'ty', partners('ty', 2))])  2.18 us
  transfers between devices with their start and end apart: 14, of which 4 were waited for; matrix products, arithmetic and copies ran while one was open for 0% of the time, Pallas kernels for 31%

commit v1 on v0

--- a/solution.py
+++ b/solution.py
@@ -317,7 +317,7 @@
 
 def middle_kernel(kinds_tx, n_dp, x6_in, u6_in, own_columns, factors, *rest):
     got_tx, rest = rest[:kinds_tx], rest[kinds_tx:]
-    shards, rest = rest[:n_dp], rest[n_dp:]
+    shards, rest = rest[n_dp - 2 : n_dp] + rest[: n_dp - 2], rest[n_dp:]
     x6, u6, h6, gp2, filters_ref, w_one, w_up, beside_pre = rest[:8]
     columns, beside6, beside_hidden, hidden_rims, edge_cells = rest[8:13]
     pres, grads = rest[13:15], rest[15:17]
@@ -421,7 +421,7 @@
         flat(up2[near:far]), joined(flat(h6[near - 1 : far - 1]), flat(h6[near:far]))
     )
     (before, factor_before), (after, factor_after) = tx_sides(got_tx, height)
-    got_rows = sides("ty", [ref[...].astype(F32) for ref in got_ty[::-1]])
+    got_rows = sides("ty", [ref[...].astype(F32) for ref in got_ty])
     lines = []
     for side, planes in enumerate(got_rows):
         for array, target in enumerate((xe, ue)):
@@ -804,7 +804,7 @@
             transcendentals=height * breadth * channels,
         ),
         name="middle_rows",
-    )(x6, u6, own_columns, factors, *tx_got, *shards)
+    )(x6, u6, own_columns, factors, *tx_got, *shards[2:], *shards[:2])
 
     scale = 1.0 / math.sqrt(height * breadth * n_dp * n_ty * n_tx)
     h6_edges, grad_pre_edges, kept, sent = pl.pallas_call(
@@ -824,7 +824,7 @@
         ],
         compiler_params=pltpu.CompilerParams(vmem_limit_bytes=20 * MIB),
         name="outer_rows_and_filter_grads",
-    )(x6, row_edges, edge_factors, up2, h6, gp2, w_one, w_up, *tx_got, *ty_got[::-1])
+    )(x6, row_edges, edge_factors, up2, h6, gp2, w_one, w_up, *tx_got, *ty_got)
 
     def conv_cost(macs):
         return pl.CostEstimate(

time: 46.4 us -> 46.4 us (level)
    ppermute x1, starting transfers between devices: 0.24 us -> 3.51 us  [total_by_swaps(): lax.ppermute(own, ('ty', 'tx'), both)]
    ppermute x3, starting transfers between devices: 8.13 us -> 5.3 us  [swaps(): got.append(lax.ppermute(sent[kind], axis, pairs))]
    ppermute x1, waiting for transfers between devices: 3.52 us -> 1.67 us  [total_by_swaps(): got = run_between(1, own, [lax.ppermute(own, 'ty', partners('ty', 2))])]
    ppermute x1, starting transfers between devices: 1.85 us -> 0.01 us  [total_by_swaps(): lax.ppermute(own, 'ty', partners('ty', 1))]
    ppermute x1, waiting for transfers between devices: 0.01 us -> 1.03 us  [total_by_swaps(): lax.ppermute(own, 'ty', partners('ty', 1))]
    ppermute x1, starting transfers between devices: 0.07 us -> 0.99 us  [total_by_swaps(): got = lax.ppermute(sent, 'dp', partners('dp', 1))]
    ppermute x3, waiting for transfers between devices: 0.01 us -> 0.61 us  [on_device(): lax.ppermute(shard, 'dp', partners('dp', partner))]
    ppermute x1, waiting for transfers between devices: 0.01 us -> 0.53 us  [total_by_swaps(): lax.ppermute(own, 'tx', partners('tx', 1))]
  transfers between devices with their start and end apart: 14 -> 14, of which waited for: 4 -> 7; matrix products, arithmetic and copies ran while one was open for 0% -> 0% of each run, Pallas kernels for 31% -> 31%
where the time goes in v1:
time: 46.4 us; the launch traced here: 46.2 us
  Pallas kernels  20.6 us (44%)
  starting transfers between devices  19.2 us (41%)
  waiting for transfers between devices  5.63 us (12%)
  between operations  0.74 us (2%)
    ppermute x3, starting transfers between devices, swaps(): got.append(lax.ppermute(sent[kind], axis, pairs))  5.3 us
    pallas_call x1, Pallas kernels, on_device(): pl.pallas_call(functools.partial(middle_kernel, kinds_tx, n_dp), in_specs...  4.89 us
    pallas_call x1, Pallas kernels, on_device(): pl.pallas_call(functools.partial(last_kernel, kinds, n_dp, scale), in_spe...  4.1 us
    ppermute x1, starting transfers between devices, total_by_swaps(): lax.ppermute(own, ('ty', 'tx'), both)  3.51 us
    pallas_call x1, Pallas kernels, output_step(): pl.pallas_call(output_kernel, in_specs=[VMEM] * 3, out_specs=VMEM, out_sh...  3.01 us
    pallas_call x1, Pallas kernels, grad_input_step(): pl.pallas_call(grad_input_kernel, in_specs=[VMEM] * 2, out_specs=VMEM, ou...  2.78 us
    ppermute x1, starting transfers between devices, total_by_swaps(): got = run_between(1, own, [lax.ppermute(own, 'ty', partners('ty', 2))])  2.66 us
    pallas_call x1, Pallas kernels, on_device(): pl.pallas_call(own_kernel, in_specs=[HBM] * 2 + [VMEM], out_specs=[VMEM]...  2.32 us
  transfers between devices with their start and end apart: 14, of which 7 were waited for; matrix products, arithmetic and copies ran while one was open for 0% of the time, Pallas kernels for 31%

profile of v1, /device:TPU:0, one launch (start us, length us, event | category | flops | bytes accessed | tf_op | source)
XLA Modules:
  0.0 46.2 jit_solution(3684894077181128318)
XLA Ops:
  0.6 1.4 %edge_columns.1 = (bf16[272,128]{1,0:T(8,128)(2,1)S(1)}, f32[64,64]{1,0:T(8,128)S(1)}, bf16[18,32,128]{2,1,0:T(8,128)(2,1)S(1)}, bf16[4,64,128]{2,1,0:T(8,128)(2,1)S(1)}) custom-call(s32[1,2]{1,0:T(1,128)} %offsets.1, bf16[1,64,64,128]{3,2,1,0:T(8,128)(2,1)} %features.3, bf16[1,64,64,128]{3,2,1,0:T(8,128)(2,1)} %upstream.3, f32[1,64,64]{2,1,0:T(8,128)} %speedup.1, ...), custom_call_target="tpu_custom_call" | custom-call | tf_op jit(solution)/shard_map/edge_columns/pallas_call | solution.py:715
  2.1 3.0 %collective-permute-start = (bf16[272,128]{1,0:T(8,128)(2,1)S(1)}, bf16[272,128]{1,0:T(8,128)(2,1)S(1)}, u32[]{:S(2)}, u32[]{:S(2)}) collective-permute-start(bf16[272,128]{1,0:T(8,128)(2,1)S(1)} %get-tuple-element.57), channel_id=1, source_target_pairs={{0,1},{1,0},{2,3},{3,2},{4,5},{5,4},{6,7},{7,6},{8,9},{9,8},{10,11... | collective-permute-start | bytes 208904 | tf_op jit(solution)/shard_map/ppermute | solution.py:40
  5.1 1.5 %collective-permute-start.1 = (bf16[18,32,128]{2,1,0:T(8,128)(2,1)S(1)}, bf16[18,32,128]{2,1,0:T(8,128)(2,1)S(1)}, u32[]{:S(2)}, u32[]{:S(2)}) collective-permute-start(bf16[18,32,128]{2,1,0:T(8,128)(2,1)S(1)} %get-tuple-element.59.rest_3_), channel_id=1, source_target_pairs={{0,16},{8,24},{16,0},{24,8},{1,17},{9,25},{17,1},{25,9},{2,18},{10... | collective-permute-start | bytes 442376 | tf_op jit(solution)/shard_map/ppermute | solution.py:735
  6.6 0.0 collective-permute-start.2
  6.6 0.6 %collective-permute-start.3 = (bf16[18,32,128]{2,1,0:T(8,128)(2,1)S(1)}, bf16[18,32,128]{2,1,0:T(8,128)(2,1)S(1)}, u32[]{:S(2)}, u32[]{:S(2)}) collective-permute-start(bf16[18,32,128]{2,1,0:T(8,128)(2,1)S(1)} %get-tuple-element.59.rest_3_), channel_id=1, source_target_pairs={{0,8},{8,0},{16,24},{24,16},{1,9},{9,1},{17,25},{25,17},{2,10},{10... | collective-permute-start | bytes 442376 | tf_op jit(solution)/shard_map/ppermute | solution.py:735
  7.2 2.3 %own_column_taps.1 = (bf16[32,64,768]{2,1,0:T(8,128)(2,1)S(1)}, bf16[32,64,768]{2,1,0:T(8,128)(2,1)S(1)}, bf16[32,64,256]{2,1,0:T(8,128)(2,1)S(1)}, f32[31,2,64,...) custom-call(bf16[1,64,64,128]{3,2,1,0:T(8,128)(2,1)} %features.3, ...), custom_call_target="tpu_custom_call" | custom-call | flops 100000 | bytes 100000 | tf_op jit(solution)/shard_map/own_column_taps/pallas_call | solution.py:740
  9.5 0.0 collective-permute-done.rest_0_
  9.5 0.2 edge_rows.1
  9.8 1.6 %collective-permute-start.4 = (bf16[5,80,128]{2,1,0:T(8,128)(2,1)S(1)}, bf16[5,80,128]{2,1,0:T(8,128)(2,1)S(1)}, u32[]{:S(2)}, u32[]{:S(2)}) collective-permute-start(bf16[5,80,128]{2,1,0:T(8,128)(2,1)S(1)} %get-tuple-element.68), channel_id=1, source_target_pairs={{0,2},{2,0},{4,6},{6,4},{1,3},{3,1},{5,7},{7,5},{8,10},{10,8},{12,... | collective-permute-start | bytes 307208 | tf_op jit(solution)/shard_map/ppermute | solution.py:40
  11.4 0.7 %collective-permute-start.5 = (bf16[5,80,128]{2,1,0:T(8,128)(2,1)S(1)}, bf16[5,80,128]{2,1,0:T(8,128)(2,1)S(1)}, u32[]{:S(2)}, u32[]{:S(2)}) collective-permute-start(bf16[5,80,128]{2,1,0:T(8,128)(2,1)S(1)} %get-tuple-element.69), channel_id=1, source_target_pairs={{2,4},{4,2},{3,5},{5,3},{10,12},{12,10},{11,13},{13,11},{18,20},{2... | collective-permute-start | bytes 307208 | tf_op jit(solution)/shard_map/ppermute | solution.py:40
  12.1 0.0 collective-permute-done.1.rest_1_
  12.1 0.6 %collective-permute-done.2.rest_2_ = bf16[18,32,128]{2,1,0:T(8,128)(2,1)S(1)} collective-permute-done((bf16[18,32,128]{2,1,0:T(8,128)(2,1)S(1)}, bf16[18,32,128]{2,1,0:T(8,128)(2,1)S(1)}, u32[]{:S(2)}, u32[]{:S(2)}) %collective-permute-start.2) | collective-permute-done | bytes 147488 | tf_op jit(solution)/shard_map/ppermute | solution.py:735
  12.7 0.0 collective-permute-done.3.rest_4_
  12.7 4.9 %middle_rows.1 = (bf16[32,64,768]{2,1,0:T(8,128)(2,1)S(1)}, bf16[32,64,768]{2,1,0:T(8,128)(2,1)S(1)}, bf16[31,64,768]{2,1,0:T(8,128)(2,1)S(1)}, bf16[32,64,256]{...) custom-call(bf16[32,64,768]{2,1,0:T(8,128)(2,1)S(1)} %get-tuple-elem, ...), custom_call_target="tpu_custom_call", output_to_operand_aliasing={{0}: (0, {}), {1}: (1, {})} | custom-call | flops 2415919104 | bytes 20971520 | tf_op jit(solution)/shard_map/middle_rows/pallas_call | solution.py:779
  17.6 0.0 collective-permute-done.4.rest_1_
  17.6 0.0 collective-permute-done.5.rest_2_
  17.6 4.1 %outer_rows_and_filter_grads.1 = (bf16[2,64,768]{2,1,0:T(8,128)(2,1)S(1)}, bf16[2,2,80,128]{3,2,1,0:T(8,128)(2,1)S(1)}, bf16[2,18,32,128]{3,2,1,0:T(8,128)(2,1)S(1)}, bf16[2,18,32,128]{3,2,1,0:T(8,128)(2,1)S(1)}) custom-call(bf16[32,64,768]{2,1,0:T(8,128)(2,1)S(1)} %get-tuple-element.61.x6, bf16[4,2,64,128]{3,2,1,0:T(8,128)(2,1)S(1)} %get-tuple-element.62.edges.row_edges, ...), custom_call_target="tpu_custom_call" | custom-call | tf_op jit(solution)/shard_map/outer_rows_and_filter_grads/pallas_call | solution.py:810
  21.7 1.0 %collective-permute-start.6 = (bf16[2,18,32,128]{3,2,1,0:T(8,128)(2,1)S(1)}, bf16[2,18,32,128]{3,2,1,0:T(8,128)(2,1)S(1)}, u32[]{:S(2)}, u32[]{:S(2)}) collective-permute-start(bf16[2,18,32,128]{3,2,1,0:T(8,128)(2,1)S(1)} %get-tuple-element.72), channel_id=1, source_target_pairs={{0,8},{8,0},{16,24},{24,16},{1,9},{9,1},{17,25},{25,17},{2,10},{10... | collective-permute-start | bytes 884744 | tf_op jit(solution)/shard_map/ppermute | solution.py:633
  22.7 1.2 %collective-permute-done.6.got = bf16[2,18,32,128]{3,2,1,0:T(8,128)(2,1)S(1)} collective-permute-done((bf16[2,18,32,128]{3,2,1,0:T(8,128)(2,1)S(1)}, bf16[2,18,32,128]{3,2,1,0:T(8,128)(2,1)S(1)}, u32[]{:S(2)}, u32[]{:S(2)}) %collective-permute-start.6) | collective-permute-done | bytes 294944 | tf_op jit(solution)/shard_map/ppermute | solution.py:633
  23.9 0.1 sum_on_chip.1
  24.0 1.6 %collective-permute-start.7 = (bf16[9,32,128]{2,1,0:T(8,128)(2,1)S(1)}, bf16[9,32,128]{2,1,0:T(8,128)(2,1)S(1)}, u32[]{:S(2)}, u32[]{:S(2)}) collective-permute-start(bf16[9,32,128]{2,1,0:T(8,128)(2,1)S(1)} %get-tuple-element.76), channel_id=1, source_target_pairs={{0,17},{1,16},{8,25},{9,24},{16,1},{17,0},{24,9},{25,8},{2,19},{3,... | collective-permute-start | bytes 221192 | tf_op jit(solution)/shard_map/ppermute | solution.py:644
  25.6 0.3 collective-permute-start.8
  25.9 1.7 %collective-permute-start.9 = (bf16[9,32,128]{2,1,0:T(8,128)(2,1)S(1)}, bf16[9,32,128]{2,1,0:T(8,128)(2,1)S(1)}, u32[]{:S(2)}, u32[]{:S(2)}) collective-permute-start(bf16[9,32,128]{2,1,0:T(8,128)(2,1)S(1)} %get-tuple-element.78), channel_id=1, source_target_pairs={{0,1},{1,0},{2,3},{3,2},{4,5},{5,4},{6,7},{7,6},{8,9},{9,8},{10,11... | collective-permute-start | bytes 221192 | tf_op jit(solution)/shard_map/ppermute | solution.py:646
  27.6 3.0 %output.1 = bf16[1,64,64,128]{3,2,1,0:T(8,128)(2,1)} custom-call(bf16[31,64,768]{2,1,0:T(8,128)(2,1)S(1)} %get-tuple-element.60.h6.middle, bf16[2,64,768]{2,1,0:T(8,128)(2,1)S(1)} %get-tuple-element.74.edges, bf16[18,128,128]{2,1,0:T(8,128)(2,1)S(1)} %get-tuple-element.75.filters), custom_call_target="tpu_custom_call" | custom-call | flops 1207959552 | bytes 2097152 | tf_op jit(solution)/shard_map/output/pallas_call | solution.py:838
  30.6 0.0 collective-permute-done.7.refs_1_
  30.6 0.5 %collective-permute-done.8.refs_2_ = bf16[9,32,128]{2,1,0:T(8,128)(2,1)S(1)} collective-permute-done((bf16[9,32,128]{2,1,0:T(8,128)(2,1)S(1)}, bf16[9,32,128]{2,1,0:T(8,128)(2,1)S(1)}, u32[]{:S(2)}, u32[]{:S(2)}) %collective-permute-start.8) | collective-permute-done | bytes 73760 | tf_op jit(solution)/shard_map/ppermute | solution.py:645
  31.1 0.1 collective-permute-done.9.refs_3_
  31.2 2.7 %collective-permute-start.10 = (bf16[9,32,128]{2,1,0:T(8,128)(2,1)S(1)}, bf16[9,32,128]{2,1,0:T(8,128)(2,1)S(1)}, u32[]{:S(2)}, u32[]{:S(2)}) collective-permute-start(bf16[9,32,128]{2,1,0:T(8,128)(2,1)S(1)} %sum_of_pieces.2.refs_0_), channel_id=1, source_target_pairs={{0,4},{2,6},{4,0},{6,2},{1,5},{3,7},{5,1},{7,3},{8,12},{10,14},{12... | collective-permute-start | bytes 221192 | tf_op jit(solution)/shard_map/ppermute | solution.py:650
  33.9 1.0 %grad_pre_taps.1 = (bf16[33,64,768]{2,1,0:T(8,128)(2,1)S(1)}, bf16[2,768,256]{2,1,0:T(8,128)(2,1)S(1)}) custom-call(bf16[32,64,256]{2,1,0:T(8,128)(2,1)S(1)} %get-tuple-element.65.gp2, bf16[2,2,80,128]{3,2,1,0:T(8,128)(2,1)S(1)} %get-tuple-element.84.edges, bf16[18,128,128]{2,1,0:T(8,128)(2,1)S(1)} %get-tuple-element.75.filters, ...), custom_call_target="tpu_custom_call" | custom-call | bytes 2097152 | tf_op jit(solution)/shard_map/grad_pre_taps/pallas_call | solution.py:851
  34.9 1.7 %collective-permute-done.10.refs_1_ = bf16[9,32,128]{2,1,0:T(8,128)(2,1)S(1)} collective-permute-done((bf16[9,32,128]{2,1,0:T(8,128)(2,1)S(1)}, bf16[9,32,128]{2,1,0:T(8,128)(2,1)S(1)}, u32[]{:S(2)}, u32[]{:S(2)}) %collective-permute-start.10) | collective-permute-done | bytes 73760 | tf_op jit(solution)/shard_map/ppermute | solution.py:650
  36.6 3.5 %collective-permute-start.11 = (bf16[9,32,128]{2,1,0:T(8,128)(2,1)S(1)}, bf16[9,32,128]{2,1,0:T(8,128)(2,1)S(1)}, u32[]{:S(2)}, u32[]{:S(2)}) collective-permute-start(bf16[9,32,128]{2,1,0:T(8,128)(2,1)S(1)} %sum_of_pieces.3.own), channel_id=1, source_target_pairs={{0,3},{1,2},{2,1},{3,0},{4,7},{5,6},{6,5},{7,4},{8,11},{9,10},{10,... | collective-permute-start | bytes 221192 | tf_op jit(solution)/shard_map/ppermute | solution.py:654
  40.1 1.0 %collective-permute-start.12 = (bf16[9,32,128]{2,1,0:T(8,128)(2,1)S(1)}, bf16[9,32,128]{2,1,0:T(8,128)(2,1)S(1)}, u32[]{:S(2)}, u32[]{:S(2)}) collective-permute-start(bf16[9,32,128]{2,1,0:T(8,128)(2,1)S(1)} %sum_of_pieces.3.own), channel_id=1, source_target_pairs={{0,1},{1,0},{2,3},{3,2},{4,5},{5,4},{6,7},{7,6},{8,9},{9,8},{10,11... | collective-permute-start | bytes 221192 | tf_op jit(solution)/shard_map/ppermute | solution.py:655
  41.1 0.0 collective-permute-start.13
  41.1 2.8 %grad_input.1 = bf16[1,64,64,128]{3,2,1,0:T(8,128)(2,1)} custom-call(bf16[33,64,768]{2,1,0:T(8,128)(2,1)S(1)} %get-tuple-element.90.taps6, bf16[2,768,256]{2,1,0:T(8,128)(2,1)S(1)} %get-tuple-element.91.weights), custom_call_target="tpu_custom_call" | custom-call | flops 1207959552 | bytes 2097152 | tf_op jit(solution)/shard_map/grad_input/pallas_call | solution.py:865
  43.9 0.0 collective-permute-done.11.by_both
  43.9 0.5 %collective-permute-done.12.by_x = bf16[9,32,128]{2,1,0:T(8,128)(2,1)S(1)} collective-permute-done((bf16[9,32,128]{2,1,0:T(8,128)(2,1)S(1)}, bf16[9,32,128]{2,1,0:T(8,128)(2,1)S(1)}, u32[]{:S(2)}, u32[]{:S(2)}) %collective-permute-start.12) | collective-permute-done | bytes 73760 | tf_op jit(solution)/shard_map/ppermute | solution.py:655
  44.4 1.0 %collective-permute-done.13.by_y = bf16[9,32,128]{2,1,0:T(8,128)(2,1)S(1)} collective-permute-done((bf16[9,32,128]{2,1,0:T(8,128)(2,1)S(1)}, bf16[9,32,128]{2,1,0:T(8,128)(2,1)S(1)}, u32[]{:S(2)}, u32[]{:S(2)}) %collective-permute-start.13) | collective-permute-done | bytes 73760 | tf_op jit(solution)/shard_map/ppermute | solution.py:656
  45.5 0.7 %both_halves.1 = (f32[9,32,128]{2,1,0:T(8,128)}, f32[9,32,128]{2,1,0:T(8,128)}) custom-call(bf16[9,32,128]{2,1,0:T(8,128)(2,1)S(1)} %sum_of_pieces.3.own, bf16[9,32,128]{2,1,0:T(8,128)(2,1)S(1)} %collective-permute-done.11.by_both, bf16[9,32,128]{2,1,0:T(8,128)(2,1)S(1)} %collective-permute-done.12.by_x, bf16[9,32,128]{2,1,0:T(8,128)(2,1)S(1)} %collective-permute-done.13.by_y), custom_call_target="tpu_custom_call" | custom-call | tf_op jit(solution)/shard_map/both_halves/pallas_call | solution.py:659
  (2 shorter events, 0.1 us)
Async XLA Ops:
  2.1 7.5 %collective-permute-start = (bf16[272,128]{1,0:T(8,128)(2,1)S(1)}, bf16[272,128]{1,0:T(8,128)(2,1)S(1)}, u32[]{:S(2)}, u32[]{:S(2)}) collective-permute-start(bf16[272,128]{1,0:T(8,128)(2,1)S(1)} %get-tuple-element.57), channel_id=1, source_target_pairs={{0,1},{1,0},{2,3},{3,2},{4,5},{5,4},{6,7},{7,6},{8,9},{9,8},{10,11... | collective-permute-start | bytes 208904 | tf_op jit(solution)/shard_map/ppermute | solution.py:40
  5.1 7.0 %collective-permute-start.1 = (bf16[18,32,128]{2,1,0:T(8,128)(2,1)S(1)}, bf16[18,32,128]{2,1,0:T(8,128)(2,1)S(1)}, u32[]{:S(2)}, u32[]{:S(2)}) collective-permute-start(bf16[18,32,128]{2,1,0:T(8,128)(2,1)S(1)} %get-tuple-element.59.rest_3_), channel_id=1, source_target_pairs={{0,16},{8,24},{16,0},{24,8},{1,17},{9,25},{17,1},{25,9},{2,18},{10... | collective-permute-start | bytes 442376 | tf_op jit(solution)/shard_map/ppermute | solution.py:735
  6.6 6.1 %collective-permute-start.2 = (bf16[18,32,128]{2,1,0:T(8,128)(2,1)S(1)}, bf16[18,32,128]{2,1,0:T(8,128)(2,1)S(1)}, u32[]{:S(2)}, u32[]{:S(2)}) collective-permute-start(bf16[18,32,128]{2,1,0:T(8,128)(2,1)S(1)} %get-tuple-element.59.rest_3_), channel_id=1, source_target_pairs={{0,24},{8,16},{16,8},{24,0},{1,25},{9,17},{17,9},{25,1},{2,26},{10... | collective-permute-start | bytes 442376 | tf_op jit(solution)/shard_map/ppermute | solution.py:735
  6.6 6.1 %collective-permute-start.3 = (bf16[18,32,128]{2,1,0:T(8,128)(2,1)S(1)}, bf16[18,32,128]{2,1,0:T(8,128)(2,1)S(1)}, u32[]{:S(2)}, u32[]{:S(2)}) collective-permute-start(bf16[18,32,128]{2,1,0:T(8,128)(2,1)S(1)} %get-tuple-element.59.rest_3_), channel_id=1, source_target_pairs={{0,8},{8,0},{16,24},{24,16},{1,9},{9,1},{17,25},{25,17},{2,10},{10... | collective-permute-start | bytes 442376 | tf_op jit(solution)/shard_map/ppermute | solution.py:735
  9.8 7.8 %collective-permute-start.4 = (bf16[5,80,128]{2,1,0:T(8,128)(2,1)S(1)}, bf16[5,80,128]{2,1,0:T(8,128)(2,1)S(1)}, u32[]{:S(2)}, u32[]{:S(2)}) collective-permute-start(bf16[5,80,128]{2,1,0:T(8,128)(2,1)S(1)} %get-tuple-element.68), channel_id=1, source_target_pairs={{0,2},{2,0},{4,6},{6,4},{1,3},{3,1},{5,7},{7,5},{8,10},{10,8},{12,... | collective-permute-start | bytes 307208 | tf_op jit(solution)/shard_map/ppermute | solution.py:40
  11.4 6.2 %collective-permute-start.5 = (bf16[5,80,128]{2,1,0:T(8,128)(2,1)S(1)}, bf16[5,80,128]{2,1,0:T(8,128)(2,1)S(1)}, u32[]{:S(2)}, u32[]{:S(2)}) collective-permute-start(bf16[5,80,128]{2,1,0:T(8,128)(2,1)S(1)} %get-tuple-element.69), channel_id=1, source_target_pairs={{2,4},{4,2},{3,5},{5,3},{10,12},{12,10},{11,13},{13,11},{18,20},{2... | collective-permute-start | bytes 307208 | tf_op jit(solution)/shard_map/ppermute | solution.py:40
  21.7 2.2 %collective-permute-start.6 = (bf16[2,18,32,128]{3,2,1,0:T(8,128)(2,1)S(1)}, bf16[2,18,32,128]{3,2,1,0:T(8,128)(2,1)S(1)}, u32[]{:S(2)}, u32[]{:S(2)}) collective-permute-start(bf16[2,18,32,128]{3,2,1,0:T(8,128)(2,1)S(1)} %get-tuple-element.72), channel_id=1, source_target_pairs={{0,8},{8,0},{16,24},{24,16},{1,9},{9,1},{17,25},{25,17},{2,10},{10... | collective-permute-start | bytes 884744 | tf_op jit(solution)/shard_map/ppermute | solution.py:633
  24.0 6.6 %collective-permute-start.7 = (bf16[9,32,128]{2,1,0:T(8,128)(2,1)S(1)}, bf16[9,32,128]{2,1,0:T(8,128)(2,1)S(1)}, u32[]{:S(2)}, u32[]{:S(2)}) collective-permute-start(bf16[9,32,128]{2,1,0:T(8,128)(2,1)S(1)} %get-tuple-element.76), channel_id=1, source_target_pairs={{0,17},{1,16},{8,25},{9,24},{16,1},{17,0},{24,9},{25,8},{2,19},{3,... | collective-permute-start | bytes 221192 | tf_op jit(solution)/shard_map/ppermute | solution.py:644
  25.6 5.5 %collective-permute-start.8 = (bf16[9,32,128]{2,1,0:T(8,128)(2,1)S(1)}, bf16[9,32,128]{2,1,0:T(8,128)(2,1)S(1)}, u32[]{:S(2)}, u32[]{:S(2)}) collective-permute-start(bf16[9,32,128]{2,1,0:T(8,128)(2,1)S(1)} %get-tuple-element.77), channel_id=1, source_target_pairs={{0,16},{8,24},{16,0},{24,8},{1,17},{9,25},{17,1},{25,9},{2,18},{10... | collective-permute-start | bytes 221192 | tf_op jit(solution)/shard_map/ppermute | solution.py:645
  25.9 5.3 %collective-permute-start.9 = (bf16[9,32,128]{2,1,0:T(8,128)(2,1)S(1)}, bf16[9,32,128]{2,1,0:T(8,128)(2,1)S(1)}, u32[]{:S(2)}, u32[]{:S(2)}) collective-permute-start(bf16[9,32,128]{2,1,0:T(8,128)(2,1)S(1)} %get-tuple-element.78), channel_id=1, source_target_pairs={{0,1},{1,0},{2,3},{3,2},{4,5},{5,4},{6,7},{7,6},{8,9},{9,8},{10,11... | collective-permute-start | bytes 221192 | tf_op jit(solution)/shard_map/ppermute | solution.py:646
  31.2 5.3 %collective-permute-start.10 = (bf16[9,32,128]{2,1,0:T(8,128)(2,1)S(1)}, bf16[9,32,128]{2,1,0:T(8,128)(2,1)S(1)}, u32[]{:S(2)}, u32[]{:S(2)}) collective-permute-start(bf16[9,32,128]{2,1,0:T(8,128)(2,1)S(1)} %sum_of_pieces.2.refs_0_), channel_id=1, source_target_pairs={{0,4},{2,6},{4,0},{6,2},{1,5},{3,7},{5,1},{7,3},{8,12},{10,14},{12... | collective-permute-start | bytes 221192 | tf_op jit(solution)/shard_map/ppermute | solution.py:650
  36.6 7.3 %collective-permute-start.11 = (bf16[9,32,128]{2,1,0:T(8,128)(2,1)S(1)}, bf16[9,32,128]{2,1,0:T(8,128)(2,1)S(1)}, u32[]{:S(2)}, u32[]{:S(2)}) collective-permute-start(bf16[9,32,128]{2,1,0:T(8,128)(2,1)S(1)} %sum_of_pieces.3.own), channel_id=1, source_target_pairs={{0,3},{1,2},{2,1},{3,0},{4,7},{5,6},{6,5},{7,4},{8,11},{9,10},{10,... | collective-permute-start | bytes 221192 | tf_op jit(solution)/shard_map/ppermute | solution.py:654
  40.1 4.4 %collective-permute-start.12 = (bf16[9,32,128]{2,1,0:T(8,128)(2,1)S(1)}, bf16[9,32,128]{2,1,0:T(8,128)(2,1)S(1)}, u32[]{:S(2)}, u32[]{:S(2)}) collective-permute-start(bf16[9,32,128]{2,1,0:T(8,128)(2,1)S(1)} %sum_of_pieces.3.own), channel_id=1, source_target_pairs={{0,1},{1,0},{2,3},{3,2},{4,5},{5,4},{6,7},{7,6},{8,9},{9,8},{10,11... | collective-permute-start | bytes 221192 | tf_op jit(solution)/shard_map/ppermute | solution.py:655
  41.1 4.4 %collective-permute-start.13 = (bf16[9,32,128]{2,1,0:T(8,128)(2,1)S(1)}, bf16[9,32,128]{2,1,0:T(8,128)(2,1)S(1)}, u32[]{:S(2)}, u32[]{:S(2)}) collective-permute-start(bf16[9,32,128]{2,1,0:T(8,128)(2,1)S(1)} %sum_of_pieces.3.own), channel_id=1, source_target_pairs={{0,2},{2,0},{4,6},{6,4},{1,3},{3,1},{5,7},{7,5},{8,10},{10,8},{12,... | collective-permute-start | bytes 221192 | tf_op jit(solution)/shard_map/ppermute | solution.py:656

commit v2 on v1

--- a/solution.py
+++ b/solution.py
@@ -116,10 +116,10 @@
     heads, tails = [], []
     for array in range(2):
         copies[3 + 2 * array].wait()
-        spread[...] = blocks[2 * array].astype(F32).reshape(height * RIM, channels)
+        spread[: height * RIM] = blocks[2 * array].astype(F32).reshape(height * RIM, channels)
         heads += [column(0), column(1)]
         copies[4 + 2 * array].wait()
-        spread[...] = blocks[2 * array + 1].astype(F32).reshape(height * RIM, channels)
+        spread[: height * RIM] = blocks[2 * array + 1].astype(F32).reshape(height * RIM, channels)
         tails += [column(RIM - 2), column(RIM - 1)]
     across = jnp.transpose(factor)
     heads.append(factor_tile(across[:1], channels))
@@ -421,7 +421,7 @@
         flat(up2[near:far]), joined(flat(h6[near - 1 : far - 1]), flat(h6[near:far]))
     )
     (before, factor_before), (after, factor_after) = tx_sides(got_tx, height)
-    got_rows = sides("ty", [ref[...].astype(F32) for ref in got_ty])
+    got_rows = sides("ty", [ref[...].astype(F32) for ref in got_ty[::-1]])
     lines = []
     for side, planes in enumerate(got_rows):
         for array, target in enumerate((xe, ue)):
@@ -655,7 +655,6 @@
         lax.ppermute(own, "tx", partners("tx", 1)),
         lax.ppermute(own, "ty", partners("ty", 1)),
     ]
-    got = run_between(2, own, got)
     return pl.pallas_call(
         halves_kernel,
         in_specs=[VMEM] * 4,
@@ -696,7 +695,6 @@
     )(got)
     (total,) = run_between(0, shared, [lax.all_to_all(shared, ("ty", "tx"), 0, 0, tiled=True)])
     run_between(1, shared, [total])
-    run_between(2, shared, [total])
     total = total.astype(F32).reshape(2, taps // 2, mine, channels)
     return total[0], total[1]
 
@@ -720,7 +718,7 @@
         + [pltpu.VMEM((height, breadth), F32), pltpu.VMEM((2 * taps, mine, channels), BF16)]
         + [pltpu.VMEM((4, height, channels), BF16)],
         scratch_shapes=[
-            pltpu.VMEM((height * RIM, channels), F32),
+            pltpu.VMEM(((height + 1) * RIM, channels), F32),
             pltpu.VMEM((4, height, RIM, channels), BF16),
             pltpu.VMEM(speedup.shape, F32),
             pltpu.VMEM(land_mask.shape, jnp.int32),
@@ -824,7 +822,7 @@
         ],
         compiler_params=pltpu.CompilerParams(vmem_limit_bytes=20 * MIB),
         name="outer_rows_and_filter_grads",
-    )(x6, row_edges, edge_factors, up2, h6, gp2, w_one, w_up, *tx_got, *ty_got)
+    )(x6, row_edges, edge_factors, up2, h6, gp2, w_one, w_up, *tx_got, *ty_got[::-1])
 
     def conv_cost(macs):
         return pl.CostEstimate(
@@ -875,7 +873,11 @@
     results = []
 
     def run_between(which, ready, got):
-        result = (output_step, taps_step, grad_input_step)[which](ready)
+        if which == 0:
+            result = output_step(ready)
+        else:
+            results.append(taps_step(ready))
+            result = grad_input_step(ready)
         result, got = lax.optimization_barrier((result, got))
         results.append(result)
         return got

time: 46.4 us -> 45.8 us (0.987)
  starting transfers between devices: 19.2 us -> 18.4 us
    ppermute x1, starting transfers between devices: 3.51 us -> 0.4 us  [total_by_swaps(): lax.ppermute(own, ('ty', 'tx'), both)]
    ppermute x3, starting transfers between devices: 5.3 us -> 8.13 us  [swaps(): got.append(lax.ppermute(sent[kind], axis, pairs))]
    ppermute x1, waiting for transfers between devices: 0.01 us -> 2.27 us  [total_by_swaps(): lax.ppermute(own, ('ty', 'tx'), both)]
    ppermute x1, starting transfers between devices: 0.01 us -> 1.88 us  [total_by_swaps(): lax.ppermute(own, 'ty', partners('ty', 1))]
    ppermute x1, starting transfers between devices: 2.66 us -> 0.95 us  [total_by_swaps(): got = run_between(1, own, [lax.ppermute(own, 'ty', partners('ty', 2))])]
    ppermute x1, starting transfers between devices: 0.99 us -> 0.07 us  [total_by_swaps(): got = lax.ppermute(sent, 'dp', partners('dp', 1))]
    ppermute x1, waiting for transfers between devices: 1.03 us -> 0.21 us  [total_by_swaps(): lax.ppermute(own, 'ty', partners('ty', 1))]
    ppermute x3, waiting for transfers between devices: 0.61 us -> 0.01 us  [on_device(): lax.ppermute(shard, 'dp', partners('dp', partner))]
  transfers between devices with their start and end apart: 14 -> 14, of which waited for: 7 -> 6; matrix products, arithmetic and copies ran while one was open for 0% -> 0% of each run, Pallas kernels for 31% -> 31%
where the time goes in v2:
time: 45.8 us; the launch traced here: 45.6 us
  Pallas kernels  20.6 us (45%)
  starting transfers between devices  18.4 us (40%)
  waiting for transfers between devices  5.83 us (13%)
  between operations  0.74 us (2%)
    ppermute x3, starting transfers between devices, swaps(): got.append(lax.ppermute(sent[kind], axis, pairs))  8.13 us
    pallas_call x1, Pallas kernels, on_device(): pl.pallas_call(functools.partial(middle_kernel, kinds_tx, n_dp), in_specs...  4.89 us
    pallas_call x1, Pallas kernels, on_device(): pl.pallas_call(functools.partial(last_kernel, kinds, n_dp, scale), in_spe...  4.1 us
    pallas_call x1, Pallas kernels, output_step(): pl.pallas_call(output_kernel, in_specs=[VMEM] * 3, out_specs=VMEM, out_sh...  3.01 us
    pallas_call x1, Pallas kernels, grad_input_step(): pl.pallas_call(grad_input_kernel, in_specs=[VMEM] * 2, out_specs=VMEM, ou...  2.79 us
    pallas_call x1, Pallas kernels, on_device(): pl.pallas_call(own_kernel, in_specs=[HBM] * 2 + [VMEM], out_specs=[VMEM]...  2.32 us
    ppermute x1, waiting for transfers between devices, total_by_swaps(): lax.ppermute(own, ('ty', 'tx'), both)  2.27 us
    ppermute x3, starting transfers between devices, on_device(): lax.ppermute(shard, 'dp', partners('dp', partner))  2.14 us
  transfers between devices with their start and end apart: 14, of which 6 were waited for; matrix products, arithmetic and copies ran while one was open for 0% of the time, Pallas kernels for 31%

profile of v2, /device:TPU:0, one launch (start us, length us, event | category | flops | bytes accessed | tf_op | source)
XLA Modules:
  0.0 45.6 jit_solution(1653133478096300991)
XLA Ops:
  0.6 1.4 %edge_columns.1 = (bf16[272,128]{1,0:T(8,128)(2,1)S(1)}, f32[64,64]{1,0:T(8,128)S(1)}, bf16[18,32,128]{2,1,0:T(8,128)(2,1)S(1)}, bf16[4,64,128]{2,1,0:T(8,128)(2,1)S(1)}) custom-call(s32[1,2]{1,0:T(1,128)} %offsets.1, bf16[1,64,64,128]{3,2,1,0:T(8,128)(2,1)} %features.3, bf16[1,64,64,128]{3,2,1,0:T(8,128)(2,1)} %upstream.3, f32[1,64,64]{2,1,0:T(8,128)} %speedup.1, ...), custom_call_target="tpu_custom_call" | custom-call | tf_op jit(solution)/shard_map/edge_columns/pallas_call | solution.py:713
  2.1 3.0 %collective-permute-start = (bf16[272,128]{1,0:T(8,128)(2,1)S(1)}, bf16[272,128]{1,0:T(8,128)(2,1)S(1)}, u32[]{:S(2)}, u32[]{:S(2)}) collective-permute-start(bf16[272,128]{1,0:T(8,128)(2,1)S(1)} %get-tuple-element.52), channel_id=1, source_target_pairs={{0,1},{1,0},{2,3},{3,2},{4,5},{5,4},{6,7},{7,6},{8,9},{9,8},{10,11... | collective-permute-start | bytes 208904 | tf_op jit(solution)/shard_map/ppermute | solution.py:40
  5.1 1.5 %collective-permute-start.1 = (bf16[18,32,128]{2,1,0:T(8,128)(2,1)S(1)}, bf16[18,32,128]{2,1,0:T(8,128)(2,1)S(1)}, u32[]{:S(2)}, u32[]{:S(2)}) collective-permute-start(bf16[18,32,128]{2,1,0:T(8,128)(2,1)S(1)} %get-tuple-element.54.rest_3_), channel_id=1, source_target_pairs={{0,16},{8,24},{16,0},{24,8},{1,17},{9,25},{17,1},{25,9},{2,18},{10... | collective-permute-start | bytes 442376 | tf_op jit(solution)/shard_map/ppermute | solution.py:733
  6.6 0.0 collective-permute-start.2
  6.6 0.6 %collective-permute-start.3 = (bf16[18,32,128]{2,1,0:T(8,128)(2,1)S(1)}, bf16[18,32,128]{2,1,0:T(8,128)(2,1)S(1)}, u32[]{:S(2)}, u32[]{:S(2)}) collective-permute-start(bf16[18,32,128]{2,1,0:T(8,128)(2,1)S(1)} %get-tuple-element.54.rest_3_), channel_id=1, source_target_pairs={{0,8},{8,0},{16,24},{24,16},{1,9},{9,1},{17,25},{25,17},{2,10},{10... | collective-permute-start | bytes 442376 | tf_op jit(solution)/shard_map/ppermute | solution.py:733
  7.2 2.3 %own_column_taps.1 = (bf16[32,64,768]{2,1,0:T(8,128)(2,1)S(1)}, bf16[32,64,768]{2,1,0:T(8,128)(2,1)S(1)}, bf16[32,64,256]{2,1,0:T(8,128)(2,1)S(1)}, f32[31,2,64,...) custom-call(bf16[1,64,64,128]{3,2,1,0:T(8,128)(2,1)} %features.3, ...), custom_call_target="tpu_custom_call" | custom-call | flops 100000 | bytes 100000 | tf_op jit(solution)/shard_map/own_column_taps/pallas_call | solution.py:738
  9.5 0.0 collective-permute-done.rest_0_
  9.5 0.2 edge_rows.1
  9.8 0.7 %collective-permute-start.4 = (bf16[5,80,128]{2,1,0:T(8,128)(2,1)S(1)}, bf16[5,80,128]{2,1,0:T(8,128)(2,1)S(1)}, u32[]{:S(2)}, u32[]{:S(2)}) collective-permute-start(bf16[5,80,128]{2,1,0:T(8,128)(2,1)S(1)} %get-tuple-element.63), channel_id=1, source_target_pairs={{2,4},{4,2},{3,5},{5,3},{10,12},{12,10},{11,13},{13,11},{18,20},{2... | collective-permute-start | bytes 307208 | tf_op jit(solution)/shard_map/ppermute | solution.py:40
  10.5 4.5 %collective-permute-start.5 = (bf16[5,80,128]{2,1,0:T(8,128)(2,1)S(1)}, bf16[5,80,128]{2,1,0:T(8,128)(2,1)S(1)}, u32[]{:S(2)}, u32[]{:S(2)}) collective-permute-start(bf16[5,80,128]{2,1,0:T(8,128)(2,1)S(1)} %get-tuple-element.64), channel_id=1, source_target_pairs={{0,2},{2,0},{4,6},{6,4},{1,3},{3,1},{5,7},{7,5},{8,10},{10,8},{12,... | collective-permute-start | bytes 307208 | tf_op jit(solution)/shard_map/ppermute | solution.py:40
  14.9 0.0 collective-permute-done.1.rest_1_
  14.9 0.0 collective-permute-done.2.rest_2_
  14.9 0.0 collective-permute-done.3.rest_4_
  14.9 4.9 %middle_rows.1 = (bf16[32,64,768]{2,1,0:T(8,128)(2,1)S(1)}, bf16[32,64,768]{2,1,0:T(8,128)(2,1)S(1)}, bf16[31,64,768]{2,1,0:T(8,128)(2,1)S(1)}, bf16[32,64,256]{...) custom-call(bf16[32,64,768]{2,1,0:T(8,128)(2,1)S(1)} %get-tuple-elem, ...), custom_call_target="tpu_custom_call", output_to_operand_aliasing={{0}: (0, {}), {1}: (1, {})} | custom-call | flops 2415919104 | bytes 20971520 | tf_op jit(solution)/shard_map/middle_rows/pallas_call | solution.py:777
  19.8 0.0 collective-permute-done.4.rest_1_
  19.9 0.0 collective-permute-done.5.rest_2_
  19.9 4.1 %outer_rows_and_filter_grads.1 = (bf16[2,64,768]{2,1,0:T(8,128)(2,1)S(1)}, bf16[2,2,80,128]{3,2,1,0:T(8,128)(2,1)S(1)}, bf16[2,18,32,128]{3,2,1,0:T(8,128)(2,1)S(1)}, bf16[2,18,32,128]{3,2,1,0:T(8,128)(2,1)S(1)}) custom-call(bf16[32,64,768]{2,1,0:T(8,128)(2,1)S(1)} %get-tuple-element.56.x6, bf16[4,2,64,128]{3,2,1,0:T(8,128)(2,1)S(1)} %get-tuple-element.57.edges.row_edges, ...), custom_call_target="tpu_custom_call" | custom-call | tf_op jit(solution)/shard_map/outer_rows_and_filter_grads/pallas_call | solution.py:808
  24.0 0.1 collective-permute-start.6
  24.1 1.6 %collective-permute-done.6.got = bf16[2,18,32,128]{3,2,1,0:T(8,128)(2,1)S(1)} collective-permute-done((bf16[2,18,32,128]{3,2,1,0:T(8,128)(2,1)S(1)}, bf16[2,18,32,128]{3,2,1,0:T(8,128)(2,1)S(1)}, u32[]{:S(2)}, u32[]{:S(2)}) %collective-permute-start.6) | collective-permute-done | bytes 294944 | tf_op jit(solution)/shard_map/ppermute | solution.py:633
  25.6 0.1 sum_on_chip.1
  25.7 1.6 %collective-permute-start.7 = (bf16[9,32,128]{2,1,0:T(8,128)(2,1)S(1)}, bf16[9,32,128]{2,1,0:T(8,128)(2,1)S(1)}, u32[]{:S(2)}, u32[]{:S(2)}) collective-permute-start(bf16[9,32,128]{2,1,0:T(8,128)(2,1)S(1)} %get-tuple-element.71), channel_id=1, source_target_pairs={{0,17},{1,16},{8,25},{9,24},{16,1},{17,0},{24,9},{25,8},{2,19},{3,... | collective-permute-start | bytes 221192 | tf_op jit(solution)/shard_map/ppermute | solution.py:644
  27.3 0.5 %collective-permute-start.8 = (bf16[9,32,128]{2,1,0:T(8,128)(2,1)S(1)}, bf16[9,32,128]{2,1,0:T(8,128)(2,1)S(1)}, u32[]{:S(2)}, u32[]{:S(2)}) collective-permute-start(bf16[9,32,128]{2,1,0:T(8,128)(2,1)S(1)} %get-tuple-element.72), channel_id=1, source_target_pairs={{0,16},{8,24},{16,0},{24,8},{1,17},{9,25},{17,1},{25,9},{2,18},{10... | collective-permute-start | bytes 221192 | tf_op jit(solution)/shard_map/ppermute | solution.py:645
  27.8 1.5 %collective-permute-start.9 = (bf16[9,32,128]{2,1,0:T(8,128)(2,1)S(1)}, bf16[9,32,128]{2,1,0:T(8,128)(2,1)S(1)}, u32[]{:S(2)}, u32[]{:S(2)}) collective-permute-start(bf16[9,32,128]{2,1,0:T(8,128)(2,1)S(1)} %get-tuple-element.73), channel_id=1, source_target_pairs={{0,1},{1,0},{2,3},{3,2},{4,5},{5,4},{6,7},{7,6},{8,9},{9,8},{10,11... | collective-permute-start | bytes 221192 | tf_op jit(solution)/shard_map/ppermute | solution.py:646
  29.3 3.0 %output.1 = bf16[1,64,64,128]{3,2,1,0:T(8,128)(2,1)} custom-call(bf16[31,64,768]{2,1,0:T(8,128)(2,1)S(1)} %get-tuple-element.55.h6.middle, bf16[2,64,768]{2,1,0:T(8,128)(2,1)S(1)} %get-tuple-element.69.edges, bf16[18,128,128]{2,1,0:T(8,128)(2,1)S(1)} %get-tuple-element.70.filters), custom_call_target="tpu_custom_call" | custom-call | flops 1207959552 | bytes 2097152 | tf_op jit(solution)/shard_map/output/pallas_call | solution.py:836
  32.3 0.0 collective-permute-done.7.refs_1_
  32.3 0.3 collective-permute-done.8.refs_2_
  32.6 0.1 collective-permute-done.9.refs_3_
  32.7 1.0 %collective-permute-start.10 = (bf16[9,32,128]{2,1,0:T(8,128)(2,1)S(1)}, bf16[9,32,128]{2,1,0:T(8,128)(2,1)S(1)}, u32[]{:S(2)}, u32[]{:S(2)}) collective-permute-start(bf16[9,32,128]{2,1,0:T(8,128)(2,1)S(1)} %sum_of_pieces.2.refs_0_), channel_id=1, source_target_pairs={{0,4},{2,6},{4,0},{6,2},{1,5},{3,7},{5,1},{7,3},{8,12},{10,14},{12... | collective-permute-start | bytes 221192 | tf_op jit(solution)/shard_map/ppermute | solution.py:650
  33.6 1.0 %grad_pre_taps.1 = (bf16[33,64,768]{2,1,0:T(8,128)(2,1)S(1)}, bf16[2,768,256]{2,1,0:T(8,128)(2,1)S(1)}) custom-call(bf16[32,64,256]{2,1,0:T(8,128)(2,1)S(1)} %get-tuple-element.60.gp2, bf16[2,2,80,128]{3,2,1,0:T(8,128)(2,1)S(1)} %get-tuple-element.79.edges, bf16[18,128,128]{2,1,0:T(8,128)(2,1)S(1)} %get-tuple-element.70.filters, ...), custom_call_target="tpu_custom_call" | custom-call | bytes 2097152 | tf_op jit(solution)/shard_map/grad_pre_taps/pallas_call | solution.py:849
  34.6 2.8 %grad_input.1 = bf16[1,64,64,128]{3,2,1,0:T(8,128)(2,1)} custom-call(bf16[33,64,768]{2,1,0:T(8,128)(2,1)S(1)} %get-tuple-element.82.taps6, bf16[2,768,256]{2,1,0:T(8,128)(2,1)S(1)} %get-tuple-element.83.weights), custom_call_target="tpu_custom_call" | custom-call | flops 1207959552 | bytes 2097152 | tf_op jit(solution)/shard_map/grad_input/pallas_call | solution.py:863
  37.4 1.4 %collective-permute-done.10.refs_1_ = bf16[9,32,128]{2,1,0:T(8,128)(2,1)S(1)} collective-permute-done((bf16[9,32,128]{2,1,0:T(8,128)(2,1)S(1)}, bf16[9,32,128]{2,1,0:T(8,128)(2,1)S(1)}, u32[]{:S(2)}, u32[]{:S(2)}) %collective-permute-start.10) | collective-permute-done | bytes 73760 | tf_op jit(solution)/shard_map/ppermute | solution.py:650
  38.8 0.4 collective-permute-start.11
  39.2 1.3 %collective-permute-start.12 = (bf16[9,32,128]{2,1,0:T(8,128)(2,1)S(1)}, bf16[9,32,128]{2,1,0:T(8,128)(2,1)S(1)}, u32[]{:S(2)}, u32[]{:S(2)}) collective-permute-start(bf16[9,32,128]{2,1,0:T(8,128)(2,1)S(1)} %sum_of_pieces.3.own), channel_id=1, source_target_pairs={{0,1},{1,0},{2,3},{3,2},{4,5},{5,4},{6,7},{7,6},{8,9},{9,8},{10,11... | collective-permute-start | bytes 221192 | tf_op jit(solution)/shard_map/ppermute | solution.py:655
  40.5 1.9 %collective-permute-start.13 = (bf16[9,32,128]{2,1,0:T(8,128)(2,1)S(1)}, bf16[9,32,128]{2,1,0:T(8,128)(2,1)S(1)}, u32[]{:S(2)}, u32[]{:S(2)}) collective-permute-start(bf16[9,32,128]{2,1,0:T(8,128)(2,1)S(1)} %sum_of_pieces.3.own), channel_id=1, source_target_pairs={{0,2},{2,0},{4,6},{6,4},{1,3},{3,1},{5,7},{7,5},{8,10},{10,8},{12,... | collective-permute-start | bytes 221192 | tf_op jit(solution)/shard_map/ppermute | solution.py:656
  42.4 2.3 %collective-permute-done.11.by_both = bf16[9,32,128]{2,1,0:T(8,128)(2,1)S(1)} collective-permute-done((bf16[9,32,128]{2,1,0:T(8,128)(2,1)S(1)}, bf16[9,32,128]{2,1,0:T(8,128)(2,1)S(1)}, u32[]{:S(2)}, u32[]{:S(2)}) %collective-permute-start.11) | collective-permute-done | bytes 73760 | tf_op jit(solution)/shard_map/ppermute | solution.py:654
  44.7 0.0 collective-permute-done.12.by_x
  44.7 0.2 collective-permute-done.13.by_y
  44.9 0.7 %both_halves.1 = (f32[9,32,128]{2,1,0:T(8,128)}, f32[9,32,128]{2,1,0:T(8,128)}) custom-call(bf16[9,32,128]{2,1,0:T(8,128)(2,1)S(1)} %sum_of_pieces.3.own, bf16[9,32,128]{2,1,0:T(8,128)(2,1)S(1)} %collective-permute-done.11.by_both, bf16[9,32,128]{2,1,0:T(8,128)(2,1)S(1)} %collective-permute-done.12.by_x, bf16[9,32,128]{2,1,0:T(8,128)(2,1)S(1)} %collective-permute-done.13.by_y), custom_call_target="tpu_custom_call" | custom-call | tf_op jit(solution)/shard_map/both_halves/pallas_call | solution.py:658
  (2 shorter events, 0.1 us)
Async XLA Ops:
  2.1 7.5 %collective-permute-start = (bf16[272,128]{1,0:T(8,128)(2,1)S(1)}, bf16[272,128]{1,0:T(8,128)(2,1)S(1)}, u32[]{:S(2)}, u32[]{:S(2)}) collective-permute-start(bf16[272,128]{1,0:T(8,128)(2,1)S(1)} %get-tuple-element.52), channel_id=1, source_target_pairs={{0,1},{1,0},{2,3},{3,2},{4,5},{5,4},{6,7},{7,6},{8,9},{9,8},{10,11... | collective-permute-start | bytes 208904 | tf_op jit(solution)/shard_map/ppermute | solution.py:40
  5.1 9.9 %collective-permute-start.1 = (bf16[18,32,128]{2,1,0:T(8,128)(2,1)S(1)}, bf16[18,32,128]{2,1,0:T(8,128)(2,1)S(1)}, u32[]{:S(2)}, u32[]{:S(2)}) collective-permute-start(bf16[18,32,128]{2,1,0:T(8,128)(2,1)S(1)} %get-tuple-element.54.rest_3_), channel_id=1, source_target_pairs={{0,16},{8,24},{16,0},{24,8},{1,17},{9,25},{17,1},{25,9},{2,18},{10... | collective-permute-start | bytes 442376 | tf_op jit(solution)/shard_map/ppermute | solution.py:733
  6.6 8.4 %collective-permute-start.2 = (bf16[18,32,128]{2,1,0:T(8,128)(2,1)S(1)}, bf16[18,32,128]{2,1,0:T(8,128)(2,1)S(1)}, u32[]{:S(2)}, u32[]{:S(2)}) collective-permute-start(bf16[18,32,128]{2,1,0:T(8,128)(2,1)S(1)} %get-tuple-element.54.rest_3_), channel_id=1, source_target_pairs={{0,24},{8,16},{16,8},{24,0},{1,25},{9,17},{17,9},{25,1},{2,26},{10... | collective-permute-start | bytes 442376 | tf_op jit(solution)/shard_map/ppermute | solution.py:733
  6.6 8.4 %collective-permute-start.3 = (bf16[18,32,128]{2,1,0:T(8,128)(2,1)S(1)}, bf16[18,32,128]{2,1,0:T(8,128)(2,1)S(1)}, u32[]{:S(2)}, u32[]{:S(2)}) collective-permute-start(bf16[18,32,128]{2,1,0:T(8,128)(2,1)S(1)} %get-tuple-element.54.rest_3_), channel_id=1, source_target_pairs={{0,8},{8,0},{16,24},{24,16},{1,9},{9,1},{17,25},{25,17},{2,10},{10... | collective-permute-start | bytes 442376 | tf_op jit(solution)/shard_map/ppermute | solution.py:733
  9.8 10.0 %collective-permute-start.4 = (bf16[5,80,128]{2,1,0:T(8,128)(2,1)S(1)}, bf16[5,80,128]{2,1,0:T(8,128)(2,1)S(1)}, u32[]{:S(2)}, u32[]{:S(2)}) collective-permute-start(bf16[5,80,128]{2,1,0:T(8,128)(2,1)S(1)} %get-tuple-element.63), channel_id=1, source_target_pairs={{2,4},{4,2},{3,5},{5,3},{10,12},{12,10},{11,13},{13,11},{18,20},{2... | collective-permute-start | bytes 307208 | tf_op jit(solution)/shard_map/ppermute | solution.py:40
  10.5 9.4 %collective-permute-start.5 = (bf16[5,80,128]{2,1,0:T(8,128)(2,1)S(1)}, bf16[5,80,128]{2,1,0:T(8,128)(2,1)S(1)}, u32[]{:S(2)}, u32[]{:S(2)}) collective-permute-start(bf16[5,80,128]{2,1,0:T(8,128)(2,1)S(1)} %get-tuple-element.64), channel_id=1, source_target_pairs={{0,2},{2,0},{4,6},{6,4},{1,3},{3,1},{5,7},{7,5},{8,10},{10,8},{12,... | collective-permute-start | bytes 307208 | tf_op jit(solution)/shard_map/ppermute | solution.py:40
  24.0 1.6 %collective-permute-start.6 = (bf16[2,18,32,128]{3,2,1,0:T(8,128)(2,1)S(1)}, bf16[2,18,32,128]{3,2,1,0:T(8,128)(2,1)S(1)}, u32[]{:S(2)}, u32[]{:S(2)}) collective-permute-start(bf16[2,18,32,128]{3,2,1,0:T(8,128)(2,1)S(1)} %get-tuple-element.67), channel_id=1, source_target_pairs={{0,8},{8,0},{16,24},{24,16},{1,9},{9,1},{17,25},{25,17},{2,10},{10... | collective-permute-start | bytes 884744 | tf_op jit(solution)/shard_map/ppermute | solution.py:633
  25.7 6.6 %collective-permute-start.7 = (bf16[9,32,128]{2,1,0:T(8,128)(2,1)S(1)}, bf16[9,32,128]{2,1,0:T(8,128)(2,1)S(1)}, u32[]{:S(2)}, u32[]{:S(2)}) collective-permute-start(bf16[9,32,128]{2,1,0:T(8,128)(2,1)S(1)} %get-tuple-element.71), channel_id=1, source_target_pairs={{0,17},{1,16},{8,25},{9,24},{16,1},{17,0},{24,9},{25,8},{2,19},{3,... | collective-permute-start | bytes 221192 | tf_op jit(solution)/shard_map/ppermute | solution.py:644
  27.3 5.3 %collective-permute-start.8 = (bf16[9,32,128]{2,1,0:T(8,128)(2,1)S(1)}, bf16[9,32,128]{2,1,0:T(8,128)(2,1)S(1)}, u32[]{:S(2)}, u32[]{:S(2)}) collective-permute-start(bf16[9,32,128]{2,1,0:T(8,128)(2,1)S(1)} %get-tuple-element.72), channel_id=1, source_target_pairs={{0,16},{8,24},{16,0},{24,8},{1,17},{9,25},{17,1},{25,9},{2,18},{10... | collective-permute-start | bytes 221192 | tf_op jit(solution)/shard_map/ppermute | solution.py:645
  27.8 4.9 %collective-permute-start.9 = (bf16[9,32,128]{2,1,0:T(8,128)(2,1)S(1)}, bf16[9,32,128]{2,1,0:T(8,128)(2,1)S(1)}, u32[]{:S(2)}, u32[]{:S(2)}) collective-permute-start(bf16[9,32,128]{2,1,0:T(8,128)(2,1)S(1)} %get-tuple-element.73), channel_id=1, source_target_pairs={{0,1},{1,0},{2,3},{3,2},{4,5},{5,4},{6,7},{7,6},{8,9},{9,8},{10,11... | collective-permute-start | bytes 221192 | tf_op jit(solution)/shard_map/ppermute | solution.py:646
  32.7 6.1 %collective-permute-start.10 = (bf16[9,32,128]{2,1,0:T(8,128)(2,1)S(1)}, bf16[9,32,128]{2,1,0:T(8,128)(2,1)S(1)}, u32[]{:S(2)}, u32[]{:S(2)}) collective-permute-start(bf16[9,32,128]{2,1,0:T(8,128)(2,1)S(1)} %sum_of_pieces.2.refs_0_), channel_id=1, source_target_pairs={{0,4},{2,6},{4,0},{6,2},{1,5},{3,7},{5,1},{7,3},{8,12},{10,14},{12... | collective-permute-start | bytes 221192 | tf_op jit(solution)/shard_map/ppermute | solution.py:650
  38.8 5.8 %collective-permute-start.11 = (bf16[9,32,128]{2,1,0:T(8,128)(2,1)S(1)}, bf16[9,32,128]{2,1,0:T(8,128)(2,1)S(1)}, u32[]{:S(2)}, u32[]{:S(2)}) collective-permute-start(bf16[9,32,128]{2,1,0:T(8,128)(2,1)S(1)} %sum_of_pieces.3.own), channel_id=1, source_target_pairs={{0,3},{1,2},{2,1},{3,0},{4,7},{5,6},{6,5},{7,4},{8,11},{9,10},{10,... | collective-permute-start | bytes 221192 | tf_op jit(solution)/shard_map/ppermute | solution.py:654
  39.2 5.4 %collective-permute-start.12 = (bf16[9,32,128]{2,1,0:T(8,128)(2,1)S(1)}, bf16[9,32,128]{2,1,0:T(8,128)(2,1)S(1)}, u32[]{:S(2)}, u32[]{:S(2)}) collective-permute-start(bf16[9,32,128]{2,1,0:T(8,128)(2,1)S(1)} %sum_of_pieces.3.own), channel_id=1, source_target_pairs={{0,1},{1,0},{2,3},{3,2},{4,5},{5,4},{6,7},{7,6},{8,9},{9,8},{10,11... | collective-permute-start | bytes 221192 | tf_op jit(solution)/shard_map/ppermute | solution.py:655
  40.5 4.4 %collective-permute-start.13 = (bf16[9,32,128]{2,1,0:T(8,128)(2,1)S(1)}, bf16[9,32,128]{2,1,0:T(8,128)(2,1)S(1)}, u32[]{:S(2)}, u32[]{:S(2)}) collective-permute-start(bf16[9,32,128]{2,1,0:T(8,128)(2,1)S(1)} %sum_of_pieces.3.own), channel_id=1, source_target_pairs={{0,2},{2,0},{4,6},{6,4},{1,3},{3,1},{5,7},{7,5},{8,10},{10,8},{12,... | collective-permute-start | bytes 221192 | tf_op jit(solution)/shard_map/ppermute | solution.py:656
